TPU v7x, 128 devices: a whole 4x4x4 slice. The times are simulated.
128 devices in a mesh: group: 8 (over z, x_hi), head: 16 (over x_lo, y, core).
Axes of the slice: x: 4 (x_hi: 2, x_lo: 2; x = x_hi * 2 + x_lo), y: 4, z: 4, core: 2. Of those that a mesh axis runs over, the one named last changes fastest.
Arguments:
- states: float32 [256, 32, 128, 128], P('group', 'head'), may hold values from -6 to 6
- placement: int32 [256, 1], replicated, may hold values from 0 to 31; in each aligned block of 32 rows (0 to 31, 32 to 63, ...) at most 2 rows name the same one
- queries: bfloat16 [8, 16, 8, 2, 8, 512], P('group', 'head'), may hold values from -6 to 6
- key_vectors: bfloat16 [8, 16, 8, 2, 8, 512], P('group', 'head'), may hold values from -6 to 6
- value_vectors: bfloat16 [8, 16, 8, 2, 8, 1024], P('group', 'head'), may hold values from -6 to 6
- gate_inputs: bfloat16 [8, 16, 8, 2, 8, 1024], P('group', 'head'), may hold values from -6 to 6
- write_strength: float32 [8, 16, 8, 2, 8, 8], P('group', 'head'), may hold values from 0.05 to 1
- decay_rate: float32 [8, 16, 8, 2, 8, 8], P('group', 'head'), may hold values from 0.02 to 1
- norm_gain: float32 [128], replicated, may hold values from 0.25 to 1.75
Outputs:
- decoded: bfloat16 [8, 16, 8, 2, 8, 1024], P('group', 'head')
- final_states: float32 [8, 16, 8, 2, 8, 128, 128], P('group', 'head')
Inputs may be any that keep to these rules, and one draw needn't show every extreme that they name: `placement`: among the requests of one prefill group no decode group is named more than 2 times, and some decode group exactly 2 times.
All inputs are finite; a program needn't handle non-finite values.
Results may differ from a plain program's by a relative error of at most 0.001.
Values sent between devices are 32-bit elements; how exact they have to be, the bound alone decides.
No kernel may reach another device: no remote copies, remote signals or barrier semaphores. Data moves between devices by JAX's collectives and lax.ppermute only.
A program may use at most 128 MiB of HBM per device.

v0:
```python
import math

import jax
import jax.numpy as jnp
from jax import lax
from jax.sharding import PartitionSpec as P


def from_partner(block, axis, stride):
    count = lax.axis_size(axis)
    route = []
    for low in range(count):
        high = low | 1 << stride
        if high != low and high < count:
            route += [(low, high), (high, low)]
    return lax.ppermute(block, axis, route)


def decode(
    initial,
    live_mask,
    queries,
    key_vectors,
    value_vectors,
    gate_inputs,
    write_strength,
    decay_rate,
    norm_gain,
):
    slot_count, heads, key_size, value_size = initial.shape
    step_count = queries.shape[1]
    query_f = queries.astype(jnp.float32).reshape(slot_count, step_count, heads // 2, key_size)
    query_unit = (
        query_f
        * lax.rsqrt(jnp.sum(query_f * query_f, axis=-1, keepdims=True) + 1e-06)
        / math.sqrt(key_size)
    )
    query_unit = jnp.repeat(query_unit, 2, axis=2)
    key_f = key_vectors.astype(jnp.float32).reshape(slot_count, step_count, heads // 2, key_size)
    key_unit = key_f * lax.rsqrt(jnp.sum(key_f * key_f, axis=-1, keepdims=True) + 1e-06)
    key_unit = jnp.repeat(key_unit, 2, axis=2)
    value_f = value_vectors.astype(jnp.float32).reshape(slot_count, step_count, heads, value_size)
    gate_f = gate_inputs.astype(jnp.float32).reshape(slot_count, step_count, heads, value_size)
    state = initial
    produced = []
    for step_index in range(step_count):
        state = decay_rate[:, step_index, :, None, None] * state
        predicted = jnp.einsum(
            "shi,shij->shj", key_unit[:, step_index], state, precision=lax.Precision.HIGHEST
        )
        residual = value_f[:, step_index] - predicted
        state = (
            state
            + write_strength[:, step_index, :, None, None]
            * key_unit[:, step_index, :, :, None]
            * residual[:, :, None, :]
        )
        readout = jnp.einsum(
            "shi,shij->shj", query_unit[:, step_index], state, precision=lax.Precision.HIGHEST
        )
        normed = readout * lax.rsqrt(jnp.mean(readout * readout, axis=-1, keepdims=True) + 1e-06)
        normed = normed * norm_gain * jax.nn.silu(gate_f[:, step_index])
        produced.append(normed.reshape(slot_count, heads * value_size))
    tokens = jnp.stack(produced, axis=1)
    tokens = jnp.where(live_mask[:, None, None], tokens, 0.0).astype(jnp.bfloat16)
    state = jnp.where(live_mask[:, None, None, None], state, 0.0)
    return (tokens, state)


def send_groups(blocks):
    return lax.all_to_all(blocks, "group", split_axis=0, concat_axis=0, tiled=True)


def regroup(blocks, head_index, sub_count):
    bit_count = sub_count.bit_length() - 1
    old_shape = blocks.shape
    blocks = blocks.reshape(old_shape[:2] + (2,) * bit_count + old_shape[3:])
    for bit_number in range(bit_count):
        position = 2 + bit_count - 1 - bit_number
        own_bit = head_index >> bit_number & 1
        is_upper = own_bit == 1
        lower_half = lax.index_in_dim(blocks, 0, position, keepdims=False)
        upper_half = lax.index_in_dim(blocks, 1, position, keepdims=False)
        sending = jnp.where(is_upper, lower_half, upper_half)
        keeping = jnp.where(is_upper, upper_half, lower_half)
        received = from_partner(sending, "head", bit_number)
        blocks = jnp.stack(
            [jnp.where(is_upper, received, keeping), jnp.where(is_upper, keeping, received)],
            axis=position,
        )
    return blocks.reshape(old_shape)


def local(
    states,
    placement,
    queries,
    key_vectors,
    value_vectors,
    gate_inputs,
    write_strength,
    decay_rate,
    norm_gain,
):
    n_group = lax.axis_size("group")
    n_head = lax.axis_size("head")
    sub_count = n_head // 4
    group_reqs, shard_heads, key_size, value_size = states.shape
    slot_cap = queries.shape[3]
    step_count = queries.shape[4]
    group_index = lax.axis_index("group")
    head_index = lax.axis_index("head")
    dec_groups = n_group * sub_count
    placed_all = placement[:, 0].reshape(n_group, group_reqs)
    placed_mine = lax.dynamic_index_in_dim(placed_all, group_index, 0, keepdims=False)
    one_hot = (placed_mine[:, None] == jnp.arange(dec_groups, dtype=jnp.int32)[None, :]).astype(
        jnp.int32
    )
    ranking = jnp.cumsum(one_hot, axis=0) - 1
    matched = one_hot[:, :, None] * (
        ranking[:, :, None] == jnp.arange(slot_cap, dtype=jnp.int32)
    ).astype(jnp.int32)
    source_rows = jnp.sum(matched * jnp.arange(group_reqs, dtype=jnp.int32)[:, None, None], axis=0)
    filled = jnp.sum(matched, axis=0)
    source_rows = jnp.transpose(source_rows.reshape(n_group, sub_count, slot_cap), (0, 2, 1))
    filled = jnp.transpose(filled.reshape(n_group, sub_count, slot_cap), (0, 2, 1))
    picked = jnp.take(states, source_rows, axis=0)
    outgoing = jnp.where(filled[:, :, :, None, None, None] > 0, picked, 0.0)
    arrived = regroup(send_groups(outgoing), head_index, sub_count)
    slot_count = n_group * slot_cap
    block_heads = sub_count * shard_heads
    initial = arrived.reshape(slot_count, block_heads, key_size, value_size)
    my_group = group_index * sub_count + head_index % sub_count
    counts = jnp.sum((placed_all == my_group).astype(jnp.int32), axis=1)
    live_mask = (counts[:, None] > jnp.arange(slot_cap, dtype=jnp.int32)[None, :]).reshape(
        slot_count
    )
    tokens, finals = decode(
        initial,
        live_mask,
        queries.reshape(slot_count, step_count, queries.shape[5]),
        key_vectors.reshape(slot_count, step_count, key_vectors.shape[5]),
        value_vectors.reshape(slot_count, step_count, value_vectors.shape[5]),
        gate_inputs.reshape(slot_count, step_count, gate_inputs.shape[5]),
        write_strength.reshape(slot_count, step_count, block_heads),
        decay_rate.reshape(slot_count, step_count, block_heads),
        norm_gain,
    )
    decoded = tokens.reshape(1, 1, n_group, slot_cap, step_count, block_heads * value_size)
    final_states = finals.reshape(1, 1, n_group, slot_cap, block_heads, key_size, value_size)
    return (decoded, final_states)


def solution(mesh):
    in_specs = (
        P("group", "head", None, None),
        P(),
        P("group", "head", None, None, None, None),
        P("group", "head", None, None, None, None),
        P("group", "head", None, None, None, None),
        P("group", "head", None, None, None, None),
        P("group", "head", None, None, None, None),
        P("group", "head", None, None, None, None),
        P(),
    )
    out_specs = (
        P("group", "head", None, None, None, None),
        P("group", "head", None, None, None, None, None),
    )
    return jax.shard_map(local, mesh=mesh, in_specs=in_specs, out_specs=out_specs, check_vma=False)
```

profile of v0, /device:TPU:1, one launch (start us, length us, event | category | flops | bytes accessed | tf_op | source)
XLA Modules:
  0.0 473.2 jit_solution(2720986654728970862)
XLA Ops:
  1.1 1.3 reduce.3
  3.1 6.7 %gather_fusion = f32[64,2,128,128]{3,2,1,0:T(8,128)} fusion(f32[32,2,128,128]{3,2,1,0:T(8,128)} %param.9, s32[1024]{0:T(1024)S(1)} %pad_clamp_fusion), kind=kCustom, calls=%fused_computation | custom fusion | bytes 16777472 | tf_op jit(solution)/shard_map/jit(_take)/gather | solution.py:127
  9.8 8.8 %select_select_fusion = f32[8,2,4,2,128,128]{5,4,3,2,1,0:T(8,128)} fusion(f32[8,2,4,2,128,128]{5,4,3,2,1,0:T(8,128)} %bitcast.316, pred[8,2,4]{2,1,0:T(4,128)(4,1)S(1)} %copy.180, pred[8,2,4]{2,1,0:T(4,128)(4,1)S(1)} %copy.179), kind=kLoop, calls=%fused_computation.15 | loop fusion | flops 4194304 | bytes 16777344 | tf_op jit(solution)/shard_map/jit(_where)/select_n | solution.py:128
  18.5 8.3 %all-to-all-start = ((f32[8,2,4,2,128,128]{5,4,3,2,1,0:T(8,128)}), f32[8,2,4,2,128,128]{5,4,3,2,1,0:T(8,128)}, u32[]{:S(2)}, u32[]{:S(2)}) async-start(f32[8,2,4,2,128,128]{5,4,3,2,1,0:T(8,128)} %select_select_fusion), calls=%async_computation | async-start | bytes 16777216 | tf_op jit(solution)/shard_map/all_to_all | solution.py:71
  26.9 95.0 %all-to-all-done = f32[8,2,4,2,128,128]{5,4,3,2,1,0:T(8,128)} async-done(((f32[8,2,4,2,128,128]{5,4,3,2,1,0:T(8,128)}), f32[8,2,4,2,128,128]{5,4,3,2,1,0:T(8,128)}, u32[]{:S(2)}, u32[]{:S(2)}) %all-to-all-start) | async-done | bytes 8388640 | tf_op jit(solution)/shard_map/all_to_all | solution.py:71
  121.9 6.6 %fusion.26 = f32[8,2,2,2,128,128]{5,4,3,2,1,0:T(8,128)} fusion(f32[8,2,2,2,2,128,128]{6,5,4,3,2,1,0:T(8,128)} %bitcast.12, pred[]{:T(512)S(6)} %eq.57), kind=kLoop, calls=%fused_computation.42 | loop fusion | flops 1048576 | bytes 12582913 | tf_op jit(solution)/shard_map/jit(_where)/select_n | solution.py:84
  128.5 1.9 collective-permute-start
  130.4 7.1 %collective-permute-done = f32[8,2,2,2,128,128]{5,4,3,2,1,0:T(8,128)} collective-permute-done((f32[8,2,2,2,128,128]{5,4,3,2,1,0:T(8,128)}, f32[8,2,2,2,128,128]{5,4,3,2,1,0:T(8,128)}, u32[]{:S(2)}, u32[]{:S(2)}) %collective-permute-start) | collective-permute-done | bytes 4194336 | tf_op jit(solution)/shard_map/ppermute | solution.py:16
  137.5 6.0 %fusion.29 = (f32[8,2,2,1,2,128,128]{6,5,4,2,1,0,3:T(8,128)S(1)}, f32[8,2,2,1,2,128,128]{6,5,4,2,1,0,3:T(8,128)S(1)}) fusion(f32[8,2,2,2,128,128]{5,4,3,2,1,0:T(8,128)} %collective-permute-done, pred[]{:T(512)S(6)} %eq.57, f32[8,2,2,2,2,128,128]{6,5,4,3,2,1,0:T(8,128)} %bitcast.12), kind=kLoop, calls=%fused_computation.49 | loop fusion | flops 3145728 | bytes 20972544 | tf_op jit(solution)/shard_map/stack | solution.py:87
  143.6 1.9 copy-done.1
  145.5 2.6 fusion.25
  148.2 1.3 collective-permute-start.1
  152.5 87.8 %collective-permute-done.1 = f32[8,2,2,2,128,128]{5,4,3,1,0,2:T(8,128)} collective-permute-done((f32[8,2,2,2,128,128]{5,4,3,1,0,2:T(8,128)}, f32[8,2,2,2,128,128]{5,4,3,1,0,2:T(8,128)}, u32[]{:S(2)}, u32[]{:S(2)}) %collective-permute-start.1) | collective-permute-done | bytes 4194336 | tf_op jit(solution)/shard_map/ppermute | solution.py:16
  240.3 4.9 %fusion.27 = (f32[8,2,1,2,2,128,128]{6,5,4,1,0,3,2:T(8,128)S(1)}, f32[8,2,1,2,2,128,128]{6,5,4,1,0,3,2:T(8,128)S(1)}) fusion(f32[8,2,2,2,128,128]{5,4,3,1,0,2:T(8,128)} %collective-permute-done.1, pred[]{:T(512)S(6)} %eq.56, f32[8,2,2,1,2,128,128]{6,5,4,2,1,0,3:T(8,128)} %copy-done.3, f32[8,2,2,1,2,128,128]{6,5,4,2,1,0,3:T(8,128)S(1)} %copy-done.2), kind=kLoop, calls=%fused_computation.45 | loop fusion | flops 7340032 | bytes 20972544 | tf_op jit(solution)/shard_map/stack | solution.py:87
  247.4 7.1 %fusion.18 = f32[16,8,1,128]{3,2,1,0:T(1,128)S(1)} fusion(f32[16,8,128,1]{2,3,1,0:T(1,128)S(1)} %bitcast.330, f32[16,8,128,128]{3,2,1,0:T(8,128)S(1)} %bitcast.307, f32[16,8]{1,0:T(8,128)S(1)} %bitcast.395), kind=kOutput, calls=%fused_computation.31 | convolution fusion | flops 27262976 | bytes 8520192 | tf_op jit(solution)/shard_map/shi,shij->shj/dot_general | solution.py:48
  254.6 8.3 %fusion.16 = f32[16,8,1,128]{3,2,1,0:T(1,128)S(1)} fusion(f32[16,8,128,1]{2,3,1,0:T(1,128)S(1)} %bitcast.368, f32[16,8,128,128]{3,2,1,0:T(8,128)S(1)} %bitcast.308, f32[16,8]{1,0:T(8,128)S(1)} %bitcast.421, f32[16,8,128]{2,1,0:T(8,128)S(1)} %sub.29, f32[16,8,128]{2,1,0:T(8,128)S(1)} %get-tuple-element.9, f32[16,8]{1,0:T(8,128)S(1)} %bitcast.396), kind=kOutput, calls=%fused_computation.29 | convolution fusion | flops 33554432 | bytes 8651776 | tf_op jit(solution)/shard_map/shi,shij->shj/dot_general | solution.py:48
  262.9 11.7 %fusion.14 = f32[16,8,1,128]{3,2,1,0:T(1,128)S(1)} fusion(f32[16,8,128,1]{2,3,1,0:T(1,128)S(1)} %bitcast.366, f32[16,8]{1,0:T(8,128)S(1)} %bitcast.416, f32[16,8,128,128]{3,2,1,0:T(8,128)S(1)} %bitcast.309, f32[16,8,128]{2,1,0:T(8,128)S(1)} %sub.30, f32[16,8,128]{2,1,0:T(8,128)S(1)} %get-tuple-element.10, f32[16,8]{1,0:T(8,128)S(1)} %bitcast.422, ...), kind=kOutput, calls=%fused_computation.27 | convolution fusion | flops 39845888 | bytes 8783360 | tf_op jit(solution)/shard_map/shi,shij->shj/dot_general | solution.py:48
  274.6 15.6 %fusion.12 = f32[16,8,1,128]{3,2,1,0:T(1,128)S(1)} fusion(f32[16,8,128,1]{2,3,1,0:T(1,128)S(1)} %bitcast.364, f32[16,8]{1,0:T(8,128)S(1)} %bitcast.413, f32[16,8,128]{2,1,0:T(8,128)S(1)} %sub.31, f32[16,8,128]{2,1,0:T(8,128)S(1)} %get-tuple-element.11, f32[16,8]{1,0:T(8,128)S(1)} %bitcast.417, f32[16,8,128,128]{3,2,1,0:T(8,128)S(1)} %bitcast.310, ...), kind=kOutput, calls=%fused_computation.25 | convolution fusion | flops 46137344 | bytes 8914944 | tf_op jit(solution)/shard_map/shi,shij->shj/dot_general | solution.py:48
  290.1 13.0 %multiply_add_fusion.3 = f32[16,8,128,128]{3,2,1,0:T(8,128)S(1)} fusion(f32[16,8,128]{2,1,0:T(8,128)S(1)} %sub.32, f32[16,8,128]{2,1,0:T(8,128)S(1)} %get-tuple-element.12, f32[16,8]{1,0:T(8,128)S(1)} %bitcast.414, f32[16,8,128]{2,1,0:T(8,128)S(1)} %sub.31, f32[16,8,128]{2,1,0:T(8,128)S(1)} %get-tuple-element.11, f32[16,8]{1,0:T(8,128)S(1)} %bitcast.418, ...), kind=kLoop, calls=%fused_computation.11 | loop fusion | flops 25165824 | bytes 17303552 | tf_op jit(solution)/shard_map/add | solution.py:53
  303.2 7.1 %fusion.10 = f32[16,8,1,128]{3,2,1,0:T(1,128)S(1)} fusion(f32[16,8,128,1]{2,3,1,0:T(1,128)S(1)} %bitcast.328, f32[16,8,128,128]{3,2,1,0:T(8,128)S(1)} %multiply_add_fusion.3, f32[16,8]{1,0:T(8,128)S(1)} %bitcast.404), kind=kOutput, calls=%fused_computation.23 | convolution fusion | flops 27262976 | bytes 8520192 | tf_op jit(solution)/shard_map/shi,shij->shj/dot_general | solution.py:48
  310.3 8.3 %fusion.8 = f32[16,8,1,128]{3,2,1,0:T(1,128)S(1)} fusion(f32[16,8,128,1]{2,3,1,0:T(1,128)S(1)} %bitcast.362, f32[16,8,128,128]{3,2,1,0:T(8,128)S(1)} %multiply_add_fusion.3, f32[16,8]{1,0:T(8,128)S(1)} %bitcast.465, f32[16,8,128]{2,1,0:T(8,128)S(1)} %sub.33, f32[16,8,128]{2,1,0:T(8,128)S(1)} %get-tuple-element.13, f32[16,8]{1,0:T(8,128)S(1)} %bitcast.405), kind=kOutput, calls=%fused_computation.21 | convolution fusion | flops 33554432 | bytes 8651776 | tf_op jit(solution)/shard_map/shi,shij->shj/dot_general | solution.py:48
  318.6 11.7 %fusion.6 = f32[16,8,1,128]{3,2,1,0:T(1,128)S(1)} fusion(f32[16,8,128,1]{2,3,1,0:T(1,128)S(1)} %bitcast.360, f32[16,8]{1,0:T(8,128)S(1)} %bitcast.460, f32[16,8,128,128]{3,2,1,0:T(8,128)S(1)} %multiply_add_fusion.3, f32[16,8,128]{2,1,0:T(8,128)S(1)} %sub.34, f32[16,8,128]{2,1,0:T(8,128)S(1)} %get-tuple-element.14, f32[16,8]{1,0:T(8,128)S(1)} %bitcast.466, ...), kind=kOutput, calls=%fused_computation.19 | convolution fusion | flops 39845888 | bytes 8783360 | tf_op jit(solution)/shard_map/shi,shij->shj/dot_general | solution.py:48
  330.3 15.4 %fusion.23 = f32[16,8,1,128]{3,2,1,0:T(1,128)S(1)} fusion(f32[16,8,128,1]{2,3,1,0:T(1,128)S(1)} %bitcast.448, f32[16,8,128]{2,1,0:T(8,128)S(1)} %sub.35, f32[16,8,128]{2,1,0:T(8,128)S(1)} %get-tuple-element.15, f32[16,8]{1,0:T(8,128)S(1)} %bitcast.461, f32[16,8,128,128]{3,2,1,0:T(8,128)S(1)} %multiply_add_fusion.3, f32[16,8,128]{2,1,0:T(8,128)S(1)} %sub.34, ...), kind=kOutput, calls=%fused_computation.36 | convolution fusion | flops 44040192 | bytes 8914432 | tf_op jit(solution)/shard_map/shi,shij->shj/dot_general | solution.py:58
  345.9 7.9 %fusion.20 = f32[16,8,1,128]{3,2,1,0:T(1,128)S(1)} fusion(f32[16,8,128,1]{2,3,1,0:T(1,128)S(1)} %bitcast.346, f32[16,8,128,128]{3,2,1,0:T(8,128)S(1)} %bitcast.312, f32[16,8,128]{2,1,0:T(8,128)S(1)} %sub.29, f32[16,8,128]{2,1,0:T(8,128)S(1)} %get-tuple-element.9, f32[16,8]{1,0:T(8,128)S(1)} %bitcast.400), kind=kOutput, calls=%fused_computation.33 | convolution fusion | flops 31457280 | bytes 8651264 | tf_op jit(solution)/shard_map/shi,shij->shj/dot_general | solution.py:58
  353.9 15.6 %fusion.4 = f32[16,8,1,128]{3,2,1,0:T(1,128)S(1)} fusion(f32[16,8,128,1]{2,3,1,0:T(1,128)S(1)} %bitcast.358, f32[16,8]{1,0:T(8,128)S(1)} %bitcast.457, f32[16,8,128]{2,1,0:T(8,128)S(1)} %sub.35, f32[16,8,128]{2,1,0:T(8,128)S(1)} %get-tuple-element.15, f32[16,8]{1,0:T(8,128)S(1)} %bitcast.462, f32[16,8,128,128]{3,2,1,0:T(8,128)S(1)} %multiply_add_fusion.3, ...), kind=kOutput, calls=%fused_computation.17 | convolution fusion | flops 46137344 | bytes 8914944 | tf_op jit(solution)/shard_map/shi,shij->shj/dot_general | solution.py:48
  369.4 21.0 %fusion = f32[16,8,1,128]{3,2,1,0:T(1,128)S(1)} fusion(f32[16,8,128,1]{2,3,1,0:T(1,128)S(1)} %bitcast.447, f32[16,8,128]{2,1,0:T(8,128)S(1)} %sub.36, f32[16,8,128]{2,1,0:T(8,128)S(1)} %get-tuple-element.8, f32[16,8]{1,0:T(8,128)S(1)} %bitcast.458, f32[16,8,128]{2,1,0:T(8,128)S(1)} %sub.35, f32[16,8,128]{2,1,0:T(8,128)S(1)} %get-tuple-element.15, ...), kind=kOutput, calls=%fused_computation.5 | convolution fusion | flops 50331648 | bytes 9046016 | tf_op jit(solution)/shard_map/shi,shij->shj/dot_general | solution.py:58
  390.5 11.5 %fusion.75 = f32[16,8,1,128]{3,2,1,0:T(1,128)S(1)} fusion(f32[16,8,128,1]{2,3,1,0:T(1,128)S(1)} %bitcast.446, f32[16,8,128,128]{3,2,1,0:T(8,128)S(1)} %multiply_add_fusion.3, f32[16,8,128]{2,1,0:T(8,128)S(1)} %sub.34, f32[16,8,128]{2,1,0:T(8,128)S(1)} %get-tuple-element.14, f32[16,8]{1,0:T(8,128)S(1)} %bitcast.470, f32[16,8,128]{2,1,0:T(8,128)S(1)} %sub.33, ...), kind=kOutput, calls=%fused_computation.156 | convolution fusion | flops 37748736 | bytes 8782848 | tf_op jit(solution)/shard_map/shi,shij->shj/dot_general | solution.py:58
  402.1 11.5 %fusion.74 = f32[16,8,1,128]{3,2,1,0:T(1,128)S(1)} fusion(f32[16,8,128,1]{2,3,1,0:T(1,128)S(1)} %bitcast.445, f32[16,8,128,128]{3,2,1,0:T(8,128)S(1)} %bitcast.313, f32[16,8,128]{2,1,0:T(8,128)S(1)} %sub.30, f32[16,8,128]{2,1,0:T(8,128)S(1)} %get-tuple-element.10, f32[16,8]{1,0:T(8,128)S(1)} %bitcast.425, f32[16,8,128]{2,1,0:T(8,128)S(1)} %sub.29, ...), kind=kOutput, calls=%fused_computation.155 | convolution fusion | flops 37748736 | bytes 8782848 | tf_op jit(solution)/shard_map/shi,shij->shj/dot_general | solution.py:58
  413.6 15.6 %fusion.21 = f32[16,8,1,128]{3,2,1,0:T(1,128)S(1)} fusion(f32[16,8,128,1]{2,3,1,0:T(1,128)S(1)} %bitcast.444, f32[16,8,128]{2,1,0:T(8,128)S(1)} %sub.31, f32[16,8,128]{2,1,0:T(8,128)S(1)} %get-tuple-element.11, f32[16,8]{1,0:T(8,128)S(1)} %bitcast.419, f32[16,8,128,128]{3,2,1,0:T(8,128)S(1)} %bitcast.314, f32[16,8,128]{2,1,0:T(8,128)S(1)} %sub.30, ...), kind=kOutput, calls=%fused_computation.34 | convolution fusion | flops 44040192 | bytes 8914432 | tf_op jit(solution)/shard_map/shi,shij->shj/dot_general | solution.py:58
  429.5 7.3 %fusion.82 = f32[16,8,1,128]{3,2,1,0:T(1,128)S(1)} fusion(f32[16,8,128,1]{2,3,1,0:T(1,128)S(1)} %bitcast.345, f32[16,8,128,128]{3,2,1,0:T(8,128)S(1)} %multiply_add_fusion.3), kind=kOutput, calls=%fused_computation.163 | convolution fusion | flops 25165824 | bytes 8519680 | tf_op jit(solution)/shard_map/shi,shij->shj/dot_general | solution.py:58
  436.8 8.1 %fusion.22 = f32[16,8,1,128]{3,2,1,0:T(1,128)S(1)} fusion(f32[16,8,128,1]{2,3,1,0:T(1,128)S(1)} %bitcast.344, f32[16,8,128,128]{3,2,1,0:T(8,128)S(1)} %multiply_add_fusion.3, f32[16,8,128]{2,1,0:T(8,128)S(1)} %sub.33, f32[16,8,128]{2,1,0:T(8,128)S(1)} %get-tuple-element.13, f32[16,8]{1,0:T(8,128)S(1)} %bitcast.411), kind=kOutput, calls=%fused_computation.35 | convolution fusion | flops 31457280 | bytes 8651264 | tf_op jit(solution)/shard_map/shi,shij->shj/dot_general | solution.py:58
  447.1 25.6 %add_select_fusion = f32[1,1,8,2,8,128,128]{6,5,4,3,2,1,0:T(8,128)} fusion(f32[1,1,8,2,8,128,128]{6,5,4,3,2,1,0:T(8,128)} %bitcast.315, f32[8,2,8,128]{3,2,1,0:T(8,128)S(1)} %bitcast.343, f32[8,2,8,128]{3,2,1,0:T(8,128)S(1)} %get-tuple-element.80, f32[8,2,8,128]{3,2,1,0:T(8,128)S(1)} %bitcast.342, f32[8,2,8,128]{3,2,1,0:T(8,128)S(1)} %get-tuple-element.81, ...), kind=kLoop, calls=%fused_computation.4 | loop fusion | flops 52428800 | bytes 17829904 | tf_op jit(solution)/shard_map/jit(_where)/select_n | solution.py:66
  (87 shorter events, 8.9 us)
Async XLA Ops:
  18.5 103.4 %all-to-all-start = ((f32[8,2,4,2,128,128]{5,4,3,2,1,0:T(8,128)}), f32[8,2,4,2,128,128]{5,4,3,2,1,0:T(8,128)}, u32[]{:S(2)}, u32[]{:S(2)}) async-start(f32[8,2,4,2,128,128]{5,4,3,2,1,0:T(8,128)} %select_select_fusion), calls=%async_computation | async-start | bytes 16777216 | tf_op jit(solution)/shard_map/all_to_all | solution.py:71
  128.5 9.0 %collective-permute-start = (f32[8,2,2,2,128,128]{5,4,3,2,1,0:T(8,128)}, f32[8,2,2,2,128,128]{5,4,3,2,1,0:T(8,128)}, u32[]{:S(2)}, u32[]{:S(2)}) collective-permute-start(f32[8,2,2,2,128,128]{5,4,3,2,1,0:T(8,128)} %fusion.26), channel_id=1, source_target_pairs={{0,1},{1,0},{2,3},{3,2},{4,5},{5,4},{6,7},{7,6},{8,9},{9,8},{10,11... | collective-permute-start | bytes 12582920 | tf_op jit(solution)/shard_map/ppermute | solution.py:16
  143.6 2.0 copy-start.1
  143.6 4.6 copy-start.3
  143.6 5.9 %copy-start.6 = (bf16[1,1,8,2,8,512]{5,4,3,2,1,0:T(8,128)(2,1)S(1)}, bf16[1,1,8,2,8,512]{5,4,3,2,1,0:T(8,128)(2,1)}, u32[]{:S(2)}) copy-start(bf16[1,1,8,2,8,512]{5,4,3,2,1,0:T(8,128)(2,1)} %param.11) | copy-start | bytes 393220
  143.6 6.3 %copy-start.7 = (bf16[1,1,8,2,8,512]{5,4,3,2,1,0:T(8,128)(2,1)S(1)}, bf16[1,1,8,2,8,512]{5,4,3,2,1,0:T(8,128)(2,1)}, u32[]{:S(2)}) copy-start(bf16[1,1,8,2,8,512]{5,4,3,2,1,0:T(8,128)(2,1)} %param.12) | copy-start | bytes 393220
  143.6 6.9 %copy-start.8 = (f32[1,1,8,2,8,8]{5,4,3,2,1,0:T(8,128)S(1)}, f32[1,1,8,2,8,8]{5,4,3,2,1,0:T(8,128)}, u32[]{:S(2)}) copy-start(f32[1,1,8,2,8,8]{5,4,3,2,1,0:T(8,128)} %param.16) | copy-start | bytes 12292
  143.6 6.9 %copy-start.9 = (f32[1,1,8,2,8,8]{5,4,3,2,1,0:T(8,128)S(1)}, f32[1,1,8,2,8,8]{5,4,3,2,1,0:T(8,128)}, u32[]{:S(2)}) copy-start(f32[1,1,8,2,8,8]{5,4,3,2,1,0:T(8,128)} %param.15) | copy-start | bytes 12292
  145.5 6.2 %copy-start.4 = (bf16[1,1,8,2,8,1024]{5,4,3,2,1,0:T(8,128)(2,1)S(1)}, bf16[1,1,8,2,8,1024]{5,4,3,2,1,0:T(8,128)(2,1)}, u32[]{:S(2)}) copy-start(bf16[1,1,8,2,8,1024]{5,4,3,2,1,0:T(8,128)(2,1)} %param.14) | copy-start | bytes 786436
  145.5 6.6 %copy-start.5 = (bf16[1,1,8,2,8,1024]{5,4,3,2,1,0:T(8,128)(2,1)S(1)}, bf16[1,1,8,2,8,1024]{5,4,3,2,1,0:T(8,128)(2,1)}, u32[]{:S(2)}) copy-start(bf16[1,1,8,2,8,1024]{5,4,3,2,1,0:T(8,128)(2,1)} %param.13) | copy-start | bytes 786436
  148.2 92.1 %collective-permute-start.1 = (f32[8,2,2,2,128,128]{5,4,3,1,0,2:T(8,128)}, f32[8,2,2,2,128,128]{5,4,3,1,0,2:T(8,128)}, u32[]{:S(2)}, u32[]{:S(2)}) collective-permute-start(f32[8,2,2,2,128,128]{5,4,3,1,0,2:T(8,128)} %fusion.25), channel_id=1, source_target_pairs={{0,2},{2,0},{1,3},{3,1},{4,6},{6,4},{5,7},{7,5},{8,10},{10,8},{9,1... | collective-permute-start | bytes 12582920 | tf_op jit(solution)/shard_map/ppermute | solution.py:16
  150.3 90.0 %copy-start.2 = (f32[8,2,2,1,2,128,128]{6,5,4,2,1,0,3:T(8,128)S(1)}, f32[8,2,2,1,2,128,128]{6,5,4,2,1,0,3:T(8,128)}, u32[]{:S(2)}) copy-start(f32[8,2,2,1,2,128,128]{6,5,4,2,1,0,3:T(8,128)} %copy-done.1) | copy-start | bytes 12582916
  247.4 166.2 %copy-start = (f32[8,2,2,2,2,128,128]{6,5,4,3,2,1,0:T(8,128)}, f32[8,2,2,2,2,128,128]{6,5,4,3,2,1,0:T(8,128)S(1)}, u32[]{:S(2)}) copy-start(f32[8,2,2,2,2,128,128]{6,5,4,3,2,1,0:T(8,128)S(1)} %copy.190) | copy-start | bytes 25165828
  429.5 15.7 %copy-start.10 = (f32[128]{0:T(128)S(1)}, f32[128]{0:T(128)}, u32[]{:S(2)}) copy-start(f32[128]{0:T(128)} %param.17) | copy-start | bytes 1540
where the time goes:
time: 480 us; the launch traced here: 473 us
  waiting for transfers between devices  190 us (40%)
  matrix products  184 us (38%)
  other arithmetic  73.6 us (15%)
  local copies, waits for them, and re-layouts  12.8 us (3%)
  starting transfers between devices  11.5 us (2%)
    dot_general x8, matrix products, decode(): jnp.einsum('shi,shij->shj', query_unit[:, step_index], state, precision=l...  98.4 us
    all_to_all x1, waiting for transfers between devices, send_groups(): lax.all_to_all(blocks, 'group', split_axis=0, concat_axis=0, tiled=True)  95 us
    ppermute x2, waiting for transfers between devices, from_partner(): return lax.ppermute(block, axis, route)  94.9 us
    dot_general x8, matrix products, decode(): jnp.einsum('shi,shij->shj', key_unit[:, step_index], state, precision=lax...  85.3 us
    select_n x1, other arithmetic, decode(): state = jnp.where(live_mask[:, None, None, None], state, 0.0)  25.6 us
    add x1, other arithmetic, decode(): state + write_strength[:, step_index, :, None, None] * key_unit[:, step_i...  13 us
    another operation x3, other arithmetic, regroup(): jnp.stack([jnp.where(is_upper, received, keeping), jnp.where(is_upper, ke...  12 us
  transfers between devices with their start and end apart: 3, of which 3 were waited for; matrix products, arithmetic and copies ran while one was open for 1% of the time, Pallas kernels for 0%

commit v1 on v0

v1 whole, which is shorter than its diff:
```python
import math

import jax
import jax.numpy as jnp
from jax import lax
from jax.experimental import pallas as pl
from jax.experimental.pallas import tpu as pltpu
from jax.sharding import Mesh
from jax.sharding import PartitionSpec as P

SUBGROUPS = 4
SLOT_CAP = 2
EPS = 1e-06


def pack_kernel(n_group, reqs, placed, states, cells, live, count, sems):
    group = lax.axis_index("group")
    mine = group * SUBGROUPS + lax.axis_index("sub")
    dec_groups = n_group * SUBGROUPS

    def clear(d, carry):
        count[d] = 0
        return carry

    lax.fori_loop(0, dec_groups, clear, 0)

    def copy(r):
        d = placed[group * reqs + r]
        rank = count[d]
        count[d] = rank + 1
        return pltpu.make_async_copy(states.at[r], cells.at[d, rank], sems.at[r])

    def send(r, carry):
        copy(r).start()
        return carry

    lax.fori_loop(0, reqs, send, 0)

    for s in range(n_group):

        def tally(r, total, s=s):
            return total + jnp.where(placed[s * reqs + r] == mine, 1, 0)

        live[s] = lax.fori_loop(0, reqs, tally, 0, unroll=8)

    def drain(r, carry):
        pltpu.make_async_copy(states.at[r], cells.at[0, 0], sems.at[r]).wait()
        return carry

    lax.fori_loop(0, reqs, drain, 0)


def pack(placed, states, n_group):
    reqs, heads, key_size, value_size = states.shape
    cells = (n_group * SUBGROUPS, SLOT_CAP, heads, key_size, value_size)
    return pl.pallas_call(
        lambda *refs: pack_kernel(n_group, reqs, *refs),
        out_shape=(
            jax.ShapeDtypeStruct(cells, states.dtype),
            jax.ShapeDtypeStruct((n_group,), jnp.int32),
        ),
        in_specs=[
            pl.BlockSpec(memory_space=pltpu.SMEM),
            pl.BlockSpec(memory_space=pl.ANY),
        ],
        out_specs=(
            pl.BlockSpec(memory_space=pl.ANY),
            pl.BlockSpec(memory_space=pltpu.SMEM),
        ),
        scratch_shapes=[
            pltpu.SMEM((n_group * SUBGROUPS,), jnp.int32),
            pltpu.SemaphoreType.DMA((reqs,)),
        ],
    )(placed, states)


def split(x):
    high = x.astype(jnp.bfloat16)
    return high, (x - high.astype(jnp.float32)).astype(jnp.bfloat16)


def pair(left, right, shape):
    return jnp.concatenate(
        [jnp.broadcast_to(left, shape), jnp.broadcast_to(right, shape)], axis=1
    )


def key_head(first, second, query, key, value, gate, strength, decay, gain):
    steps, size = key.shape
    half = (steps, first.shape[1])
    state = jnp.concatenate([first, second], axis=1)
    both = jnp.concatenate([key, query], axis=0)
    key_f, query_f = key.astype(jnp.float32), query.astype(jnp.float32)
    key_norm = lax.rsqrt(jnp.sum(key_f * key_f, axis=1, keepdims=True) + EPS)
    query_norm = lax.rsqrt(jnp.sum(query_f * query_f, axis=1, keepdims=True) + EPS) / math.sqrt(size)
    high, low = split(state)
    product = jnp.dot(
        jnp.concatenate([both, both], axis=1),
        jnp.concatenate([high, low], axis=0),
        preferred_element_type=jnp.float32,
    )
    gram = lax.dot_general(
        both, key, (((1,), (1,)), ((), ())), preferred_element_type=jnp.float32
    )
    decay_w = pair(decay[:, 0:1], decay[:, 1:2], half)
    norm_w = jnp.broadcast_to(key_norm, (steps, 2 * half[1]))
    write_w = pair(strength[:, 0:1], strength[:, 1:2], half) * norm_w
    row = lax.broadcasted_iota(jnp.int32, (steps, 2 * half[1]), 0)
    writes = jnp.zeros((steps, 2 * half[1]), jnp.float32)
    readout = writes
    kept = jnp.ones((1, 2 * half[1]), jnp.float32)
    for t in range(steps):
        fade = decay_w[t : t + 1]
        product = product * fade
        residual = value[t : t + 1] - norm_w[t : t + 1] * product[t : t + 1]
        write = write_w[t : t + 1] * residual
        product = product + gram[:, t : t + 1] * write
        readout = jnp.where(row == t, product[steps:], readout)
        writes = jnp.where(row == t, write, writes * fade)
        kept = kept * fade
    high, low = split(writes)
    update = lax.dot_general(
        jnp.concatenate([key, key], axis=0),
        jnp.concatenate([high, low], axis=0),
        (((0,), (0,)), ((), ())),
        preferred_element_type=jnp.float32,
    )
    state = kept * state + update
    readout = readout * query_norm
    halves = [readout[:, : half[1]], readout[:, half[1] :]]
    halves = [
        x * lax.rsqrt(jnp.mean(x * x, axis=1, keepdims=True) + EPS) * gain for x in halves
    ]
    token = jnp.concatenate(halves, axis=1) * (gate * jax.nn.sigmoid(gate))
    return token, state


def decode_kernel(live, cells, query, key, value, gate, strength, decay, gain, tokens, finals):
    s = pl.program_id(0)
    sources, heads = cells.shape[1], cells.shape[3]
    size, width = cells.shape[4], cells.shape[5]
    for k in range(SLOT_CAP):
        at = (0, 0, 0, k)

        @pl.when(live[s] > k)
        def _(k=k, at=at):
            for i in range(sources):
                keys = slice(i * size, (i + 1) * size)
                values = slice(i * heads * width, (i + 1) * heads * width)
                token, state = key_head(
                    cells[0, i, k, 0],
                    cells[0, i, k, 1],
                    query[at][:, keys],
                    key[at][:, keys],
                    value[at][:, values].astype(jnp.float32),
                    gate[at][:, values].astype(jnp.float32),
                    strength[at][:, heads * i : heads * (i + 1)],
                    decay[at][:, heads * i : heads * (i + 1)],
                    gain[...],
                )
                tokens[0, 0, 0, k, :, values] = token.astype(tokens.dtype)
                for a in range(heads):
                    finals[0, 0, 0, k, heads * i + a] = state[:, a * width : (a + 1) * width]

        @pl.when(live[s] <= k)
        def _(k=k):
            tokens[0, 0, 0, k] = jnp.zeros(tokens.shape[4:], tokens.dtype)
            finals[0, 0, 0, k] = jnp.zeros(finals.shape[4:], finals.dtype)


def decode(live, arrived, queries, key_vectors, value_vectors, gate_inputs, strength, decay, gain):
    n_group = queries.shape[2]
    _, cap, heads, key_size, value_size = arrived.shape
    cells = arrived.reshape(n_group, SUBGROUPS, cap, heads, key_size, value_size)
    block_heads = SUBGROUPS * heads
    out_shape = (
        jax.ShapeDtypeStruct(value_vectors.shape, jnp.bfloat16),
        jax.ShapeDtypeStruct(
            (1, 1, n_group, cap, block_heads, key_size, value_size), jnp.float32
        ),
    )

    def per_source(shape):
        block = (1, 1, 1) + shape[3:]
        return pl.BlockSpec(block, lambda s: (0, 0, s) + (0,) * (len(shape) - 3))

    return pl.pallas_call(
        decode_kernel,
        grid=(n_group,),
        out_shape=out_shape,
        in_specs=[
            pl.BlockSpec(memory_space=pltpu.SMEM),
            pl.BlockSpec((1,) + cells.shape[1:], lambda s: (s, 0, 0, 0, 0, 0)),
            per_source(queries.shape),
            per_source(key_vectors.shape),
            per_source(value_vectors.shape),
            per_source(gate_inputs.shape),
            per_source(strength.shape),
            per_source(decay.shape),
            pl.BlockSpec((1, value_size), lambda s: (0, 0)),
        ],
        out_specs=tuple(per_source(o.shape) for o in out_shape),
        compiler_params=pltpu.CompilerParams(vmem_limit_bytes=32 * 1024 * 1024),
    )(live, cells, queries, key_vectors, value_vectors, gate_inputs, strength, decay, gain)


def local(states, placement, queries, key_vectors, value_vectors, gate_inputs, strength, decay, gain):
    n_group = lax.axis_size("group")
    placed = placement.reshape(placement.shape[0])
    cells, live = pack(placed, states, n_group)
    arrived = lax.all_to_all(cells, ("group", "sub"), split_axis=0, concat_axis=0, tiled=True)
    return decode(
        live,
        arrived,
        queries,
        key_vectors,
        value_vectors,
        gate_inputs,
        strength,
        decay,
        gain.reshape(1, gain.shape[0]),
    )


def solution(mesh):
    n_group, n_head = mesh.devices.shape
    quads = Mesh(
        mesh.devices.reshape(n_group, n_head // SUBGROUPS, SUBGROUPS), ("group", "block", "sub")
    )
    spread = P("group", ("block", "sub"))
    return jax.shard_map(
        local,
        mesh=quads,
        in_specs=(spread, P(), spread, spread, spread, spread, spread, spread, P()),
        out_specs=(spread, spread),
        check_vma=False,
    )
```

time: 480 us -> 253 us (0.53)
  waiting for transfers between devices: 190 us -> 0 us
  matrix products: 184 us -> 0 us
  Pallas kernels: 0 us -> 141 us
  blocking collectives: 0 us -> 107 us
  other arithmetic: 73.6 us -> 0 us
  local copies, waits for them, and re-layouts: 12.8 us -> 0.05 us
  starting transfers between devices: 11.5 us -> 0 us
    dot_general x16 -> x0, matrix products: 184 us -> none  [the longest x8 98.4 us: decode(): jnp.einsum('shi,shij->shj', query_unit[:, step_index], state, precision=l...]
    pallas_call x0 -> x2, Pallas kernels: none -> 141 us  [the longest x1 130 us: pack(): pl.pallas_call(lambda *refs: pack_kernel(n_group, reqs, *refs), out_shape...]
    all_to_all x0 -> x1, blocking collectives: none -> 107 us  [local(): lax.all_to_all(cells, ('group', 'sub'), split_axis=0, concat_axis=0, tile...]
    all_to_all x1 -> x0, waiting for transfers between devices: 95 us -> none  [send_groups(): lax.all_to_all(blocks, 'group', split_axis=0, concat_axis=0, tiled=True)]
    ppermute x2 -> x0, waiting for transfers between devices: 94.9 us -> none  [from_partner(): return lax.ppermute(block, axis, route)]
    select_n x5 -> x0, other arithmetic: 43.6 us -> none  [the longest x1 25.6 us: decode(): state = jnp.where(live_mask[:, None, None, None], state, 0.0)]
    add x1 -> x0, other arithmetic: 13 us -> none  [decode(): state + write_strength[:, step_index, :, None, None] * key_unit[:, step_i...]
    another operation x4 -> x0, other arithmetic: 12.1 us -> none  [the longest x3 12 us: regroup(): jnp.stack([jnp.where(is_upper, received, keeping), jnp.where(is_upper, ke...]
  transfers between devices with their start and end apart: 3 -> 0, of which waited for: 3 -> 0; matrix products, arithmetic and copies ran while one was open for 1% -> 0% of each run, Pallas kernels for 0% -> 0%
where the time goes in v1:
time: 253 us; the launch traced here: 249 us
  Pallas kernels  141 us (56%)
  blocking collectives  107 us (42%)
    pallas_call x1, Pallas kernels, pack(): pl.pallas_call(lambda *refs: pack_kernel(n_group, reqs, *refs), out_shape...  130 us
    all_to_all x1, blocking collectives, local(): lax.all_to_all(cells, ('group', 'sub'), split_axis=0, concat_axis=0, tile...  107 us
    pallas_call x1, Pallas kernels, decode(): pl.pallas_call(decode_kernel, grid=(n_group,), out_shape=out_shape, in_sp...  10.7 us

profile of v1, /device:TPU:1, one launch (start us, length us, event | category | flops | bytes accessed | tf_op | source)
XLA Modules:
  0.0 248.8 jit_solution(14737581276628616400)
XLA Ops:
  0.6 129.9 %shard_map.104 = (f32[32,2,2,128,128]{4,3,2,1,0:T(8,128)}, s32[8]{0:T(128)}) custom-call(s32[256]{0:T(256)} %bitcast.5, f32[32,2,128,128]{3,2,1,0:T(8,128)} %refs_1_.1), custom_call_target="tpu_custom_call" | custom-call | tf_op jit(solution)/shard_map/pallas_call | solution.py:56
  130.5 0.0 copy-start
  130.5 0.0 copy-start.1
  130.5 0.0 copy-start.2
  130.5 0.0 copy-start.3
  130.5 0.0 copy-start.4
  130.6 0.0 copy-start.5
  130.6 0.0 copy-start.6
  130.6 0.0 copy-start.7
  130.6 107.5 %all_to_all.5 = f32[32,2,2,128,128]{4,3,2,1,0:T(8,128)S(1)} all-to-all(f32[32,2,2,128,128]{4,3,2,1,0:T(8,128)} %get-tuple-element.5), channel_id=1, replica_groups=mesh['group'=8,'block'=4,'sub'=4] {'group','sub'}, dimensions={0} | all-to-all | bytes 16777216 | tf_op jit(solution)/shard_map/all_to_all | solution.py:211
  238.1 0.0 copy-done
  238.1 0.0 copy-done.1
  238.1 0.0 copy-done.2
  238.1 0.0 copy-done.3
  238.1 0.0 copy-done.4
  238.1 0.0 copy-done.5
  238.1 0.0 copy-done.6
  238.1 0.0 copy-done.7
  238.2 10.7 %shard_map.105 = (bf16[1,1,8,2,8,1024]{5,4,3,2,1,0:T(8,128)(2,1)}, f32[1,1,8,2,8,128,128]{6,5,4,3,2,1,0:T(8,128)}) custom-call(s32[8]{0:T(128)S(1)} %copy-done.7, f32[8,4,2,2,128,128]{5,4,3,2,1,0:T(8,128)S(1)} %bitcast.3, bf16[1,1,8,2,8,512]{5,4,3,2,1,0:T(8,128)(2,1)S(1)} %copy-done.2, bf16[1,1,8,2,8,512]{5,4,3,2,1,0:T(8,128)(2,1)S(1)} %copy-done.3, ...), custom_call_target="tpu_custom_call" | custom-call | tf_op jit(solution)/shard_map/pallas_call | solution.py:187
Async XLA Ops:
  130.5 107.6 %copy-start = (bf16[1,1,8,2,8,1024]{5,4,3,2,1,0:T(8,128)(2,1)S(1)}, bf16[1,1,8,2,8,1024]{5,4,3,2,1,0:T(8,128)(2,1)}, u32[]{:S(2)}) copy-start(bf16[1,1,8,2,8,1024]{5,4,3,2,1,0:T(8,128)(2,1)} %value.1) | copy-start | bytes 786436
  130.5 107.6 %copy-start.1 = (bf16[1,1,8,2,8,1024]{5,4,3,2,1,0:T(8,128)(2,1)S(1)}, bf16[1,1,8,2,8,1024]{5,4,3,2,1,0:T(8,128)(2,1)}, u32[]{:S(2)}) copy-start(bf16[1,1,8,2,8,1024]{5,4,3,2,1,0:T(8,128)(2,1)} %gate.1) | copy-start | bytes 786436
  130.5 107.6 %copy-start.2 = (bf16[1,1,8,2,8,512]{5,4,3,2,1,0:T(8,128)(2,1)S(1)}, bf16[1,1,8,2,8,512]{5,4,3,2,1,0:T(8,128)(2,1)}, u32[]{:S(2)}) copy-start(bf16[1,1,8,2,8,512]{5,4,3,2,1,0:T(8,128)(2,1)} %query.1) | copy-start | bytes 393220
  130.5 107.6 %copy-start.3 = (bf16[1,1,8,2,8,512]{5,4,3,2,1,0:T(8,128)(2,1)S(1)}, bf16[1,1,8,2,8,512]{5,4,3,2,1,0:T(8,128)(2,1)}, u32[]{:S(2)}) copy-start(bf16[1,1,8,2,8,512]{5,4,3,2,1,0:T(8,128)(2,1)} %key.1) | copy-start | bytes 393220
  130.5 107.6 %copy-start.4 = (f32[1,1,8,2,8,8]{5,4,3,2,1,0:T(8,128)S(1)}, f32[1,1,8,2,8,8]{5,4,3,2,1,0:T(8,128)}, u32[]{:S(2)}) copy-start(f32[1,1,8,2,8,8]{5,4,3,2,1,0:T(8,128)} %strength.1) | copy-start | bytes 12292
  130.6 107.6 %copy-start.5 = (f32[1,1,8,2,8,8]{5,4,3,2,1,0:T(8,128)S(1)}, f32[1,1,8,2,8,8]{5,4,3,2,1,0:T(8,128)}, u32[]{:S(2)}) copy-start(f32[1,1,8,2,8,8]{5,4,3,2,1,0:T(8,128)} %decay.1) | copy-start | bytes 12292
  130.6 107.6 %copy-start.6 = (f32[128]{0:T(128)S(1)}, f32[128]{0:T(128)}, u32[]{:S(2)}) copy-start(f32[128]{0:T(128)} %param.17) | copy-start | bytes 1540
  130.6 107.6 %copy-start.7 = (s32[8]{0:T(128)S(1)}, s32[8]{0:T(128)}, u32[]{:S(2)}) copy-start(s32[8]{0:T(128)} %get-tuple-element.4.live) | copy-start | bytes 100

commit v2 on v1

v2 whole, which is shorter than its diff:
```python
import math

import jax
import jax.numpy as jnp
from jax import lax
from jax.experimental import pallas as pl
from jax.experimental.pallas import tpu as pltpu
from jax.sharding import Mesh
from jax.sharding import PartitionSpec as P

SUBGROUPS = 4
SLOT_CAP = 2
EPS = 1e-06


def pack_kernel(n_group, reqs, placed, states, cells, live, count, sems):
    group = lax.axis_index("group")
    mine = group * SUBGROUPS + lax.axis_index("sub")

    def clear(d, carry):
        count[d] = 0
        return carry

    lax.fori_loop(0, n_group * SUBGROUPS, clear, 0, unroll=8)

    def send(r, carry):
        d = placed[group * reqs + r]
        rank = count[d]
        count[d] = rank + 1
        pltpu.make_async_copy(states.at[r], cells.at[d, rank], sems.at[r]).start()
        return carry

    lax.fori_loop(0, reqs, send, 0, unroll=4)

    for s in range(n_group):

        def tally(r, total, s=s):
            return total + jnp.where(placed[s * reqs + r] == mine, 1, 0)

        live[s] = lax.fori_loop(0, reqs, tally, 0, unroll=8)

    def drain(r, carry):
        pltpu.make_async_copy(states.at[r], cells.at[0, 0], sems.at[r]).wait()
        return carry

    lax.fori_loop(0, reqs, drain, 0, unroll=4)


def pack(placed, states, n_group):
    reqs, heads, key_size, value_size = states.shape
    cells = (n_group * SUBGROUPS, SLOT_CAP, heads, key_size, value_size)
    return pl.pallas_call(
        lambda *refs: pack_kernel(n_group, reqs, *refs),
        out_shape=(
            pltpu.VMEM(cells, states.dtype),
            jax.ShapeDtypeStruct((n_group,), jnp.int32),
        ),
        in_specs=[
            pl.BlockSpec(memory_space=pltpu.SMEM),
            pl.BlockSpec(memory_space=pltpu.HBM),
        ],
        out_specs=(
            pl.BlockSpec(memory_space=pltpu.VMEM),
            pl.BlockSpec(memory_space=pltpu.SMEM),
        ),
        scratch_shapes=[
            pltpu.SMEM((n_group * SUBGROUPS,), jnp.int32),
            pltpu.SemaphoreType.DMA((reqs,)),
        ],
        compiler_params=pltpu.CompilerParams(vmem_limit_bytes=32 * 1024 * 1024),
    )(placed, pltpu.with_memory_space_constraint(states, pltpu.HBM))


def split(x):
    high = x.astype(jnp.bfloat16)
    return high, (x - high.astype(jnp.float32)).astype(jnp.bfloat16)


def wide(columns, width):
    return jnp.concatenate(
        [jnp.broadcast_to(c, (c.shape[0], width)) for c in columns], axis=1
    )


def decode_kernel(
    live, cells, query, key, value, gate, strength, decay, gain, tokens, finals,
    by_key, by_query, gram_key, gram_query, values, fades, writes, key_norms, kept,
):
    s = pl.program_id(0)
    sources, heads, size, width = cells.shape[1], cells.shape[3], cells.shape[4], cells.shape[5]
    steps = key.shape[4]
    units = [(k, i) for k in range(SLOT_CAP) for i in range(sources)]
    count = len(units)

    def keys(i):
        return slice(i * size, (i + 1) * size)

    def lanes(i):
        return slice(i * heads * width, (i + 1) * heads * width)

    def state_of(k, i):
        return jnp.concatenate([cells[0, i, k, a] for a in range(heads)], axis=1)

    def spread(ref, u, x):
        for a in range(heads):
            ref[a, pl.ds(u, steps, stride=count), :] = x[:, a * width : (a + 1) * width]

    def gather(ref, u):
        return jnp.concatenate(
            [ref[a, pl.ds(u, steps, stride=count), :] for a in range(heads)], axis=1
        )

    for u, (k, i) in enumerate(units):
        key_f = key[0, 0, 0, k, :, keys(i)].astype(jnp.float32)
        query_f = query[0, 0, 0, k, :, keys(i)].astype(jnp.float32)
        both = jnp.concatenate([key_f, query_f], axis=0).astype(jnp.bfloat16)
        high, low = split(state_of(k, i))
        product = jnp.dot(
            jnp.concatenate([both, both], axis=1),
            jnp.concatenate([high, low], axis=0),
            preferred_element_type=jnp.float32,
        )
        gram = lax.dot_general(
            both,
            key_f.astype(jnp.bfloat16),
            (((1,), (1,)), ((), ())),
            preferred_element_type=jnp.float32,
        )
        norm = lax.rsqrt(jnp.sum(key_f * key_f, axis=1, keepdims=True) + EPS)
        both_heads = [heads * i + a for a in range(heads)]
        spread(by_key, u, product[:steps])
        spread(by_query, u, product[steps:])
        gram_key[pl.ds(u, steps, stride=count), :] = gram[:steps]
        gram_query[pl.ds(u, steps, stride=count), :] = gram[steps:]
        spread(values, u, value[0, 0, 0, k, :, lanes(i)].astype(jnp.float32))
        spread(fades, u, wide([decay[0, 0, 0, k, :, h : h + 1] for h in both_heads], width))
        spread(
            writes, u, wide([strength[0, 0, 0, k, :, h : h + 1] * norm for h in both_heads], width)
        )
        key_norms[pl.ds(u, steps, stride=count), :] = wide([norm], width)

    def rows(t):
        return slice(t * count, (t + 1) * count)

    on_key = [[by_key[a, rows(t)] for a in range(heads)] for t in range(steps)]
    on_query = [[by_query[a, rows(t)] for a in range(heads)] for t in range(steps)]
    written, total = [], None
    for t in range(steps):
        fade = [fades[a, rows(t)] for a in range(heads)]
        total = fade if total is None else [x * f for x, f in zip(total, fade)]
        norm = key_norms[rows(t)]
        write = []
        for a in range(heads):
            residual = values[a, rows(t)] - norm * (on_key[t][a] * fade[a])
            write.append(writes[a, rows(t)] * residual)
        written = [[w * f for w, f in zip(old, fade)] for old in written] + [write]
        for later in range(t, steps):
            for on, grams in ((on_key, gram_key), (on_query, gram_query)):
                if on is on_query or later > t:
                    dot = jnp.broadcast_to(grams[rows(later)][:, t : t + 1], norm.shape)
                    on[later] = [x * f + dot * w for x, f, w in zip(on[later], fade, write)]
    kept[...] = jnp.concatenate(total, axis=1)
    for t in range(steps):
        for a in range(heads):
            by_key[a, rows(t)] = written[t][a]
            by_query[a, rows(t)] = on_query[t][a]

    for u, (k, i) in enumerate(units):
        key_f = key[0, 0, 0, k, :, keys(i)].astype(jnp.float32)
        query_f = query[0, 0, 0, k, :, keys(i)].astype(jnp.float32)
        high, low = split(gather(by_key, u))
        update = lax.dot_general(
            jnp.concatenate([key_f, key_f], axis=0).astype(jnp.bfloat16),
            jnp.concatenate([high.astype(jnp.float32), low.astype(jnp.float32)], axis=0).astype(
                jnp.bfloat16
            ),
            (((0,), (0,)), ((), ())),
            preferred_element_type=jnp.float32,
        )
        state = kept[u : u + 1, :] * state_of(k, i) + update
        for a in range(heads):
            finals[0, 0, 0, k, heads * i + a] = state[:, a * width : (a + 1) * width]
        norm = lax.rsqrt(jnp.sum(query_f * query_f, axis=1, keepdims=True) + EPS) / math.sqrt(size)
        readout = gather(by_query, u) * norm
        normed = []
        for a in range(heads):
            x = readout[:, a * width : (a + 1) * width]
            normed.append(x * lax.rsqrt(jnp.mean(x * x, axis=1, keepdims=True) + EPS) * gain[...])
        opened = gate[0, 0, 0, k, :, lanes(i)].astype(jnp.float32)
        token = jnp.concatenate(normed, axis=1) * (opened * jax.nn.sigmoid(opened))
        tokens[0, 0, 0, k, :, lanes(i)] = token.astype(tokens.dtype)

    for k in range(SLOT_CAP):

        @pl.when(live[s] <= k)
        def _(k=k):
            tokens[0, 0, 0, k] = jnp.zeros(tokens.shape[4:], tokens.dtype)
            finals[0, 0, 0, k] = jnp.zeros(finals.shape[4:], finals.dtype)


def decode(
    live, arrived, queries, key_vectors, value_vectors, gate_inputs, strength, decay, gain, space=None
):
    n_group = queries.shape[2]
    _, cap, heads, key_size, value_size = arrived.shape
    cells = arrived.reshape(n_group, SUBGROUPS, cap, heads, key_size, value_size)
    if space is not None:
        cells = pltpu.with_memory_space_constraint(cells, space)
    block_heads = SUBGROUPS * heads
    out_shape = (
        jax.ShapeDtypeStruct(value_vectors.shape, jnp.bfloat16),
        jax.ShapeDtypeStruct(
            (1, 1, n_group, cap, block_heads, key_size, value_size), jnp.float32
        ),
    )

    steps, units = queries.shape[4], cap * SUBGROUPS
    rows = steps * units
    by_step = (heads, rows, value_size)
    scratch = [by_step, by_step, (rows, steps), (rows, steps), by_step, by_step, by_step]
    scratch += [(rows, value_size), (units, heads * value_size)]

    def per_source(shape):
        block = (1, 1, 1) + shape[3:]
        return pl.BlockSpec(block, lambda s: (0, 0, s) + (0,) * (len(shape) - 3))

    return pl.pallas_call(
        decode_kernel,
        grid=(n_group,),
        out_shape=out_shape,
        in_specs=[
            pl.BlockSpec(memory_space=pltpu.SMEM),
            pl.BlockSpec((1,) + cells.shape[1:], lambda s: (s, 0, 0, 0, 0, 0)),
            per_source(queries.shape),
            per_source(key_vectors.shape),
            per_source(value_vectors.shape),
            per_source(gate_inputs.shape),
            per_source(strength.shape),
            per_source(decay.shape),
            pl.BlockSpec((1, value_size), lambda s: (0, 0)),
        ],
        out_specs=tuple(per_source(o.shape) for o in out_shape),
        scratch_shapes=[pltpu.VMEM(shape, jnp.float32) for shape in scratch],
        compiler_params=pltpu.CompilerParams(vmem_limit_bytes=32 * 1024 * 1024),
    )(live, cells, queries, key_vectors, value_vectors, gate_inputs, strength, decay, gain)


def local(states, placement, queries, key_vectors, value_vectors, gate_inputs, strength, decay, gain):
    n_group = lax.axis_size("group")
    placed = placement.reshape(placement.shape[0])
    cells, live = pack(placed, states, n_group)
    arrived = lax.all_to_all(cells, ("group", "sub"), split_axis=0, concat_axis=0, tiled=True)
    return decode(
        live,
        arrived,
        queries,
        key_vectors,
        value_vectors,
        gate_inputs,
        strength,
        decay,
        gain.reshape(1, gain.shape[0]),
    )


def solution(mesh):
    n_group, n_head = mesh.devices.shape
    quads = Mesh(
        mesh.devices.reshape(n_group, n_head // SUBGROUPS, SUBGROUPS), ("group", "block", "sub")
    )
    spread = P("group", ("block", "sub"))
    return jax.shard_map(
        local,
        mesh=quads,
        in_specs=(spread, P(), spread, spread, spread, spread, spread, spread, P()),
        out_specs=(spread, spread),
        check_vma=False,
    )
```

time: 253 us -> 122 us (0.48); the launches traced: 249 us -> 122 us
  Pallas kernels: 141 us -> 12.8 us
    pallas_call x1, Pallas kernels: 130 us -> 3.74 us  [pack(): pl.pallas_call(lambda *refs: pack_kernel(n_group, reqs, *refs), out_shape...]
where the time goes in v2:
time: 122 us
  blocking collectives  107 us (88%)
  Pallas kernels  12.8 us (10%)
    all_to_all x1, blocking collectives, local(): lax.all_to_all(cells, ('group', 'sub'), split_axis=0, concat_axis=0, tile...  107 us
    pallas_call x1, Pallas kernels, decode(): pl.pallas_call(decode_kernel, grid=(n_group,), out_shape=out_shape, in_sp...  9.08 us
    pallas_call x1, Pallas kernels, pack(): pl.pallas_call(lambda *refs: pack_kernel(n_group, reqs, *refs), out_shape...  3.74 us

profile of v2, /device:TPU:1, one launch (start us, length us, event | category | flops | bytes accessed | tf_op | source)
XLA Modules:
  0.0 121.6 jit_solution(9042741002151968312)
XLA Ops:
  0.6 0.0 copy-start.6
  0.6 0.7 copy-done.6
  1.3 3.7 %shard_map.104 = (f32[32,2,2,128,128]{4,3,2,1,0:T(8,128)S(1)}, s32[8]{0:T(128)S(1)}) custom-call(s32[256]{0:T(256)S(1)} %bitcast.4, f32[32,2,128,128]{3,2,1,0:T(8,128)} %refs_1_.1), custom_call_target="tpu_custom_call" | custom-call | tf_op jit(solution)/shard_map/pallas_call | solution.py:52
  5.1 0.0 copy-start
  5.1 0.0 copy-start.1
  5.1 0.0 copy-start.2
  5.1 0.0 copy-start.3
  5.1 0.0 copy-start.4
  5.1 0.0 copy-start.5
  5.1 0.0 copy-start.7
  5.1 107.3 %all_to_all.5 = f32[32,2,2,128,128]{4,3,2,1,0:T(8,128)S(1)} all-to-all(f32[32,2,2,128,128]{4,3,2,1,0:T(8,128)S(1)} %get-tuple-element.5), channel_id=1, replica_groups=mesh['group'=8,'block'=4,'sub'=4] {'group','sub'}, dimensions={0} | all-to-all | bytes 16777216 | tf_op jit(solution)/shard_map/all_to_all | solution.py:252
  112.4 0.0 copy-done
  112.4 0.0 copy-done.1
  112.4 0.0 copy-done.2
  112.4 0.0 copy-done.3
  112.4 0.0 copy-done.4
  112.5 0.0 copy-done.5
  112.5 0.0 copy-done.7
  112.5 9.1 %shard_map.105 = (bf16[1,1,8,2,8,1024]{5,4,3,2,1,0:T(8,128)(2,1)}, f32[1,1,8,2,8,128,128]{6,5,4,3,2,1,0:T(8,128)}) custom-call(s32[8]{0:T(128)S(1)} %get-tuple-element.4.live, f32[8,4,2,2,128,128]{5,4,3,2,1,0:T(8,128)S(1)} %bitcast.3, bf16[1,1,8,2,8,512]{5,4,3,2,1,0:T(8,128)(2,1)S(1)} %copy-done.2, bf16[1,1,8,2,8,512]{5,4,3,2,1,0:T(8,128)(2,1)S(1)} %copy-done.3, ...), custom_call_target="tpu_custom_call" | custom-call | tf_op jit(solution)/shard_map/pallas_call | solution.py:227
Async XLA Ops:
  0.6 0.7 copy-start.6
  5.1 107.4 %copy-start = (bf16[1,1,8,2,8,1024]{5,4,3,2,1,0:T(8,128)(2,1)S(1)}, bf16[1,1,8,2,8,1024]{5,4,3,2,1,0:T(8,128)(2,1)}, u32[]{:S(2)}) copy-start(bf16[1,1,8,2,8,1024]{5,4,3,2,1,0:T(8,128)(2,1)} %value.1) | copy-start | bytes 786436
  5.1 107.4 %copy-start.1 = (bf16[1,1,8,2,8,1024]{5,4,3,2,1,0:T(8,128)(2,1)S(1)}, bf16[1,1,8,2,8,1024]{5,4,3,2,1,0:T(8,128)(2,1)}, u32[]{:S(2)}) copy-start(bf16[1,1,8,2,8,1024]{5,4,3,2,1,0:T(8,128)(2,1)} %gate.1) | copy-start | bytes 786436
  5.1 107.4 %copy-start.2 = (bf16[1,1,8,2,8,512]{5,4,3,2,1,0:T(8,128)(2,1)S(1)}, bf16[1,1,8,2,8,512]{5,4,3,2,1,0:T(8,128)(2,1)}, u32[]{:S(2)}) copy-start(bf16[1,1,8,2,8,512]{5,4,3,2,1,0:T(8,128)(2,1)} %query.1) | copy-start | bytes 393220
  5.1 107.3 %copy-start.3 = (bf16[1,1,8,2,8,512]{5,4,3,2,1,0:T(8,128)(2,1)S(1)}, bf16[1,1,8,2,8,512]{5,4,3,2,1,0:T(8,128)(2,1)}, u32[]{:S(2)}) copy-start(bf16[1,1,8,2,8,512]{5,4,3,2,1,0:T(8,128)(2,1)} %key.1) | copy-start | bytes 393220
  5.1 107.3 %copy-start.4 = (f32[1,1,8,2,8,8]{5,4,3,2,1,0:T(8,128)S(1)}, f32[1,1,8,2,8,8]{5,4,3,2,1,0:T(8,128)}, u32[]{:S(2)}) copy-start(f32[1,1,8,2,8,8]{5,4,3,2,1,0:T(8,128)} %strength.1) | copy-start | bytes 12292
  5.1 107.3 %copy-start.5 = (f32[1,1,8,2,8,8]{5,4,3,2,1,0:T(8,128)S(1)}, f32[1,1,8,2,8,8]{5,4,3,2,1,0:T(8,128)}, u32[]{:S(2)}) copy-start(f32[1,1,8,2,8,8]{5,4,3,2,1,0:T(8,128)} %decay.1) | copy-start | bytes 12292
  5.1 107.3 %copy-start.7 = (f32[128]{0:T(128)S(1)}, f32[128]{0:T(128)}, u32[]{:S(2)}) copy-start(f32[128]{0:T(128)} %param.17) | copy-start | bytes 1540

commit v3 on v2

v3 whole, which is shorter than its diff:
```python
import math

import jax
import jax.numpy as jnp
from jax import lax
from jax.experimental import pallas as pl
from jax.experimental.pallas import tpu as pltpu
from jax.sharding import Mesh
from jax.sharding import PartitionSpec as P

SUBGROUPS = 4
SLOT_CAP = 2
CORES = 2
SOURCES = 2
EPS = 1e-06


def pack_kernel(n_group, reqs, spare, placed, states, cells, live, count, sems):
    group = lax.axis_index("group")
    mine = group * SUBGROUPS + lax.axis_index("sub")
    heads = states.shape[1]

    def clear(d, carry):
        count[d] = 0
        return carry

    lax.fori_loop(0, n_group * SUBGROUPS, clear, 0, unroll=8)

    def send(r, carry):
        d = placed[group * reqs + r]
        rank = count[d]
        count[d] = rank + 1
        if spare:

            @pl.when(rank == 0)
            def _():
                pltpu.make_async_copy(
                    states.at[r], cells.at[d, pl.ds(0, heads)], sems.at[r]
                ).start()

            @pl.when(rank > 0)
            def _():
                for a in range(heads):
                    pltpu.make_async_copy(
                        states.at[r, a], cells.at[d // CORES * CORES + a, heads], sems.at[r]
                    ).start()

        else:
            pltpu.make_async_copy(states.at[r], cells.at[d, rank], sems.at[r]).start()
        return carry

    lax.fori_loop(0, reqs, send, 0, unroll=4)

    for s in range(n_group):

        def tally(r, total, s=s):
            return total + jnp.where(placed[s * reqs + r] == mine, 1, 0)

        live[s] = lax.fori_loop(0, reqs, tally, 0, unroll=8)

    def drain(r, carry):
        landed = cells.at[0, pl.ds(0, heads)] if spare else cells.at[0, 0]
        pltpu.make_async_copy(states.at[r], landed, sems.at[r]).wait()
        return carry

    lax.fori_loop(0, reqs, drain, 0, unroll=4)


def pack(placed, states, n_group, spare):
    reqs, heads, key_size, value_size = states.shape
    cell = (heads + 1,) if spare else (SLOT_CAP, heads)
    cells = (n_group * SUBGROUPS,) + cell + (key_size, value_size)
    return pl.pallas_call(
        lambda *refs: pack_kernel(n_group, reqs, spare, *refs),
        out_shape=(
            pltpu.VMEM(cells, states.dtype),
            jax.ShapeDtypeStruct((n_group,), jnp.int32),
        ),
        in_specs=[
            pl.BlockSpec(memory_space=pltpu.SMEM),
            pl.BlockSpec(memory_space=pltpu.HBM),
        ],
        out_specs=(
            pl.BlockSpec(memory_space=pltpu.VMEM),
            pl.BlockSpec(memory_space=pltpu.SMEM),
        ),
        scratch_shapes=[
            pltpu.SMEM((n_group * SUBGROUPS,), jnp.int32),
            pltpu.SemaphoreType.DMA((reqs,)),
        ],
        compiler_params=pltpu.CompilerParams(vmem_limit_bytes=32 * 1024 * 1024),
    )(placed, pltpu.with_memory_space_constraint(states, pltpu.HBM))


def split(x):
    high = x.astype(jnp.bfloat16)
    return high, (x - high.astype(jnp.float32)).astype(jnp.bfloat16)


def wide(columns, width):
    return jnp.concatenate(
        [jnp.broadcast_to(c, (c.shape[0], width)) for c in columns], axis=1
    )


def decode_kernel(
    load, slot, first, live, query, key, value, gate, strength, decay, gain, tokens, finals,
    by_key, by_query, gram_key, gram_query, values, fades, writes, key_norms, kept,
):
    size, width = finals.shape[5], finals.shape[6]
    heads = finals.shape[4] // SUBGROUPS
    steps = key.shape[4]
    units = [(n, i) for n in range(SOURCES) for i in range(SUBGROUPS)]
    count = len(units)

    def keys(i):
        return slice(i * size, (i + 1) * size)

    def lanes(i):
        return slice(i * heads * width, (i + 1) * heads * width)

    def state_of(n, i):
        return jnp.concatenate(load(n, i), axis=1)

    def spread(ref, u, x):
        for a in range(heads):
            ref[a, pl.ds(u, steps, stride=count), :] = x[:, a * width : (a + 1) * width]

    def gather(ref, u):
        return jnp.concatenate(
            [ref[a, pl.ds(u, steps, stride=count), :] for a in range(heads)], axis=1
        )

    for u, (n, i) in enumerate(units):
        key_f = key[0, 0, n, 0, :, keys(i)].astype(jnp.float32)
        query_f = query[0, 0, n, 0, :, keys(i)].astype(jnp.float32)
        both = jnp.concatenate([key_f, query_f], axis=0).astype(jnp.bfloat16)
        high, low = split(state_of(n, i))
        product = jnp.dot(
            jnp.concatenate([both, both], axis=1),
            jnp.concatenate([high, low], axis=0),
            preferred_element_type=jnp.float32,
        )
        gram = lax.dot_general(
            both,
            key_f.astype(jnp.bfloat16),
            (((1,), (1,)), ((), ())),
            preferred_element_type=jnp.float32,
        )
        norm = lax.rsqrt(jnp.sum(key_f * key_f, axis=1, keepdims=True) + EPS)
        both_heads = [heads * i + a for a in range(heads)]
        spread(by_key, u, product[:steps])
        spread(by_query, u, product[steps:])
        gram_key[pl.ds(u, steps, stride=count), :] = gram[:steps]
        gram_query[pl.ds(u, steps, stride=count), :] = gram[steps:]
        spread(values, u, value[0, 0, n, 0, :, lanes(i)].astype(jnp.float32))
        spread(fades, u, wide([decay[0, 0, n, 0, :, h : h + 1] for h in both_heads], width))
        spread(
            writes, u, wide([strength[0, 0, n, 0, :, h : h + 1] * norm for h in both_heads], width)
        )
        key_norms[pl.ds(u, steps, stride=count), :] = wide([norm], width)

    def rows(t):
        return slice(t * count, (t + 1) * count)

    on_key = [[by_key[a, rows(t)] for a in range(heads)] for t in range(steps)]
    on_query = [[by_query[a, rows(t)] for a in range(heads)] for t in range(steps)]
    written, total = [], None
    for t in range(steps):
        fade = [fades[a, rows(t)] for a in range(heads)]
        total = fade if total is None else [x * f for x, f in zip(total, fade)]
        norm = key_norms[rows(t)]
        write = []
        for a in range(heads):
            residual = values[a, rows(t)] - norm * (on_key[t][a] * fade[a])
            write.append(writes[a, rows(t)] * residual)
        written = [[w * f for w, f in zip(old, fade)] for old in written] + [write]
        for later in range(t, steps):
            for on, grams in ((on_key, gram_key), (on_query, gram_query)):
                if on is on_query or later > t:
                    dot = jnp.broadcast_to(grams[rows(later)][:, t : t + 1], norm.shape)
                    on[later] = [x * f + dot * w for x, f, w in zip(on[later], fade, write)]
    kept[...] = jnp.concatenate(total, axis=1)
    for t in range(steps):
        for a in range(heads):
            by_key[a, rows(t)] = written[t][a]
            by_query[a, rows(t)] = on_query[t][a]

    for u, (n, i) in enumerate(units):
        key_f = key[0, 0, n, 0, :, keys(i)].astype(jnp.float32)
        query_f = query[0, 0, n, 0, :, keys(i)].astype(jnp.float32)
        high, low = split(gather(by_key, u))
        update = lax.dot_general(
            jnp.concatenate([key_f, key_f], axis=0).astype(jnp.bfloat16),
            jnp.concatenate([high.astype(jnp.float32), low.astype(jnp.float32)], axis=0).astype(
                jnp.bfloat16
            ),
            (((0,), (0,)), ((), ())),
            preferred_element_type=jnp.float32,
        )
        state = kept[u : u + 1, :] * state_of(n, i) + update
        for a in range(heads):
            finals[0, 0, n, 0, heads * i + a] = state[:, a * width : (a + 1) * width]
        norm = lax.rsqrt(jnp.sum(query_f * query_f, axis=1, keepdims=True) + EPS) / math.sqrt(size)
        readout = gather(by_query, u) * norm
        normed = []
        for a in range(heads):
            x = readout[:, a * width : (a + 1) * width]
            normed.append(x * lax.rsqrt(jnp.mean(x * x, axis=1, keepdims=True) + EPS) * gain[...])
        opened = gate[0, 0, n, 0, :, lanes(i)].astype(jnp.float32)
        token = jnp.concatenate(normed, axis=1) * (opened * jax.nn.sigmoid(opened))
        tokens[0, 0, n, 0, :, lanes(i)] = token.astype(tokens.dtype)

    for n in range(SOURCES):

        @pl.when(live[first + n] <= slot)
        def _(n=n):
            tokens[0, 0, n, 0] = jnp.zeros(tokens.shape[4:], tokens.dtype)
            finals[0, 0, n, 0] = jnp.zeros(finals.shape[4:], finals.dtype)


def decode(live, sources, load, slot, small, gain, earlier=None):
    queries, values = small[0], small[2]
    n_group, cap, steps = queries.shape[2:5]
    key_size, value_size = queries.shape[5] // SUBGROUPS, gain.shape[1]
    heads = values.shape[5] // (SUBGROUPS * value_size)
    out_shape = (
        jax.ShapeDtypeStruct(values.shape, jnp.bfloat16),
        jax.ShapeDtypeStruct(
            (1, 1, n_group, cap, SUBGROUPS * heads, key_size, value_size), jnp.float32
        ),
    )
    units = SOURCES * SUBGROUPS
    rows = steps * units
    by_step = (heads, rows, value_size)
    scratch = [by_step, by_step, (rows, steps), (rows, steps), by_step, by_step, by_step]
    scratch += [(rows, value_size), (units, heads * value_size)]
    groups = n_group // SOURCES

    def slot_of(j):
        return j // groups if slot is None else slot

    def per_slot(shape):
        block = (1, 1, SOURCES, 1) + shape[4:]
        return pl.BlockSpec(
            block, lambda j: (0, 0, j % groups, slot_of(j)) + (0,) * (len(shape) - 4)
        )

    def source_spec(block, index):
        return pl.BlockSpec(block, lambda j: index(j % groups, slot_of(j)))

    kept = () if earlier is None else earlier

    def kernel(live, *refs):
        blocks, refs = refs[: len(sources)], refs[len(sources) :]
        ins, refs = refs[: len(small) + 1], refs[len(small) + 1 + len(kept) :]
        j = pl.program_id(0)
        decode_kernel(
            lambda n, i: load(n, i, *blocks), slot_of(j), (j % groups) * SOURCES, live, *ins, *refs
        )

    first_kept = 1 + len(sources) + len(small) + 1
    return pl.pallas_call(
        kernel,
        grid=(groups * (cap if slot is None else 1),),
        out_shape=out_shape,
        in_specs=[pl.BlockSpec(memory_space=pltpu.SMEM)]
        + [source_spec(block, index) for _, block, index in sources]
        + [per_slot(x.shape) for x in small]
        + [pl.BlockSpec(gain.shape, lambda j: (0, 0))]
        + [pl.BlockSpec(memory_space=pl.ANY)] * len(kept),
        out_specs=tuple(per_slot(o.shape) for o in out_shape),
        scratch_shapes=[pltpu.VMEM(shape, jnp.float32) for shape in scratch],
        input_output_aliases={first_kept + n: n for n in range(len(kept))},
        compiler_params=pltpu.CompilerParams(vmem_limit_bytes=32 * 1024 * 1024),
    )(live, *[x for x, _, _ in sources], *small, gain, *kept)


def exchange(cells):
    return lax.all_to_all(cells, ("group", "sub"), split_axis=0, concat_axis=0, tiled=True)


def with_spare(placed, states, small, gain, n_group):
    cells, live = pack(placed, states, n_group, True)
    heads, key_size, value_size = states.shape[1:]
    square = (key_size, value_size)
    arrived = exchange(cells)
    spare = arrived[:, heads]
    swap = [(n, n ^ 1) for n in range(SUBGROUPS)]
    other = lax.ppermute(spare, "sub", swap)
    by_source = arrived.reshape((n_group, SUBGROUPS, heads + 1) + square)
    other = other.reshape((n_group, SUBGROUPS) + square)
    firsts = (
        by_source,
        (SOURCES, SUBGROUPS, heads) + square,
        lambda group, slot: (group, 0, 0, 0, 0),
    )
    earlier = decode(
        live, [firsts], lambda n, i, x: [x[n, i, a] for a in range(heads)], 0, small, gain
    )
    own = (by_source, (SOURCES, SUBGROUPS, 1) + square, lambda group, slot: (group, 0, heads, 0, 0))
    theirs = (other, (SOURCES, SUBGROUPS) + square, lambda group, slot: (group, 0, 0, 0))

    def load(n, i, x, y):
        core = lax.axis_index("sub") % CORES
        return [jnp.where(core == a, x[n, i, 0], y[n, i]) for a in range(heads)]

    return decode(live, [own, theirs], load, 1, small, gain, earlier)


def without_spare(placed, states, small, gain, n_group):
    cells, live = pack(placed, states, n_group, False)
    heads, key_size, value_size = states.shape[1:]
    square = (key_size, value_size)
    arrived = exchange(cells).reshape((n_group, SUBGROUPS, SLOT_CAP, heads) + square)
    block = (SOURCES, SUBGROUPS, 1, heads) + square
    slots = (arrived, block, lambda group, slot: (group, 0, slot, 0, 0, 0))
    return decode(
        live, [slots], lambda n, i, x: [x[n, i, 0, a] for a in range(heads)], None, small, gain
    )


def local(states, placement, queries, key_vectors, value_vectors, gate_inputs, strength, decay, gain):
    n_group = lax.axis_size("group")
    placed = placement.reshape(placement.shape[0])
    chips = placed.reshape(n_group, -1, 1) // CORES
    named = chips == jnp.arange(n_group * SUBGROUPS // CORES, dtype=jnp.int32)
    fits = jnp.all(jnp.sum(named.astype(jnp.int32), axis=1) <= SLOT_CAP + 1)
    small = (queries, key_vectors, value_vectors, gate_inputs, strength, decay)
    gain = gain.reshape(1, gain.shape[0])
    return lax.cond(
        fits,
        lambda *x: with_spare(*x, n_group),
        lambda *x: without_spare(*x, n_group),
        placed,
        states,
        small,
        gain,
    )


def solution(mesh):
    n_group, n_head = mesh.devices.shape
    quads = Mesh(
        mesh.devices.reshape(n_group, n_head // SUBGROUPS, SUBGROUPS), ("group", "block", "sub")
    )
    spread = P("group", ("block", "sub"))
    return jax.shard_map(
        local,
        mesh=quads,
        in_specs=(spread, P(), spread, spread, spread, spread, spread, spread, P()),
        out_specs=(spread, spread),
        check_vma=False,
    )
```

time: 122 us -> 125 us (1.025)
  other arithmetic: 0 us -> 2.21 us
    unnamed x0 -> x1, other arithmetic: none -> 1.34 us
where the time goes in v3:
time: 125 us
  blocking collectives  107 us (86%)
  Pallas kernels  13.7 us (11%)
  other arithmetic  2.21 us (2%)
  between operations  1.29 us (1%)
    all_to_all x1, blocking collectives, exchange(): lax.all_to_all(cells, ('group', 'sub'), split_axis=0, concat_axis=0, tile...  107 us
    pallas_call x1, Pallas kernels, decode(): pl.pallas_call(kernel, grid=(groups * (cap if slot is None else 1),), out...  9.83 us
    pallas_call x1, Pallas kernels, pack(): pl.pallas_call(lambda *refs: pack_kernel(n_group, reqs, spare, *refs), ou...  3.88 us

profile of v3, /device:TPU:1, one launch (start us, length us, event | category | flops | bytes accessed | tf_op | source)
XLA Modules:
  0.0 125.2 jit_solution(13710265324700702869)
XLA Ops:
  0.6 0.5 broadcast.44
  1.1 1.3 %reduce.3 = s32[256]{0:T(256)S(1)} reduce(s32[256,1]{0,1:T(1,128)} %param.12, s32[]{:T(128)} %broadcast.44), dimensions={1}, to_apply=%param.12.reduce_sub_computation.3 | reduce | bytes 2052 | tf_op args[1]
  2.5 0.1 reshape_reshape.3
  2.6 0.2 convert_reduce_fusion
  2.8 0.6 compare_reduce_fusion
  4.1 121.2 %conditional.1 = ((bf16[1,1,8,2,8,1024]{5,4,3,2,1,0:T(8,128)(2,1)}, f32[1,1,8,2,8,128,128]{6,5,4,3,2,1,0:T(8,128)})) conditional(s32[]{:T(128)} %convert_element_type.7, (s32[256,1]{0,1:T(1,128)}, f32[32,2,128,128]{3,2,1,0:T(8,128)}, bf16[1,1,8,2,8,512]{5,4,3,2,1,0:T(8,128)(2,1)}, bf16[1,1,8,2,8,512]{5,4,3,2,1,0:T(8,128)(2,1)}, ...), branch_computations={%region_2.3_spmd, %region_3.4_spmd} | conditional | bytes 28346612 | solution.py:331
  4.1 3.9 %branch_0_fun.2 = (f32[32,2,2,128,128]{4,3,2,1,0:T(8,128)S(1)}, s32[8]{0:T(128)S(1)}) custom-call(s32[256]{0:T(256)} %bitcast.14, f32[32,2,128,128]{3,2,1,0:T(8,128)} %get-tuple-element.86.refs_1_), custom_call_target="tpu_custom_call" | custom-call | tf_op jit(solution)/shard_map/cond/branch_0_fun/pallas_call | solution.py:73
  8.0 0.0 copy-start
  8.0 0.0 copy-start.2
  8.0 0.0 copy-start.4
  8.0 0.0 copy-start.6
  8.0 0.0 copy-start.8
  8.0 0.0 copy-start.10
  8.1 0.0 copy-start.12
  8.1 107.3 %all_to_all.8 = f32[32,2,2,128,128]{4,3,2,1,0:T(8,128)S(1)} all-to-all(f32[32,2,2,128,128]{4,3,2,1,0:T(8,128)S(1)} %get-tuple-element.39), channel_id=1, replica_groups=mesh['group'=8,'block'=4,'sub'=4] {'group','sub'}, dimensions={0} | all-to-all | bytes 16777216 | tf_op jit(solution)/shard_map/cond/branch_0_fun/all_to_all | solution.py:280
  115.4 0.0 copy-done
  115.4 0.0 copy-done.2
  115.4 0.0 copy-done.4
  115.4 0.0 copy-done.6
  115.4 0.0 copy-done.8
  115.4 0.0 copy-done.10
  115.4 0.0 copy-done.12
  115.4 9.8 %branch_0_fun.3 = (bf16[1,1,8,2,8,1024]{5,4,3,2,1,0:T(8,128)(2,1)}, f32[1,1,8,2,8,128,128]{6,5,4,3,2,1,0:T(8,128)}) custom-call(s32[8]{0:T(128)S(1)} %get-tuple-element.38.live, f32[8,4,2,2,128,128]{5,4,3,2,1,0:T(8,128)S(1)} %bitcast.12, bf16[1,1,8,2,8,512]{5,4,3,2,1,0:T(8,128)(2,1)S(1)} %copy-done.4, bf16[1,1,8,2,8,512]{5,4,3,2,1,0:T(8,128)(2,1)S(1)} %copy-done.6, ...), custom_call_target="tpu_custom_call" | custom-call | tf_op jit(solution)/shard_map/cond/branch_0_fun/pallas_call | solution.py:263
  (1 shorter events, 0.0 us)
Async XLA Ops:
  8.0 107.4 %copy-start = (bf16[1,1,8,2,8,1024]{5,4,3,2,1,0:T(8,128)(2,1)S(1)}, bf16[1,1,8,2,8,1024]{5,4,3,2,1,0:T(8,128)(2,1)}, u32[]{:S(2)}) copy-start(bf16[1,1,8,2,8,1024]{5,4,3,2,1,0:T(8,128)(2,1)} %get-tuple-element.92.refs_3_) | copy-start | bytes 786436 | tf_op jit(solution)/shard_map/cond
  8.0 107.4 %copy-start.2 = (bf16[1,1,8,2,8,1024]{5,4,3,2,1,0:T(8,128)(2,1)S(1)}, bf16[1,1,8,2,8,1024]{5,4,3,2,1,0:T(8,128)(2,1)}, u32[]{:S(2)}) copy-start(bf16[1,1,8,2,8,1024]{5,4,3,2,1,0:T(8,128)(2,1)} %get-tuple-element.94.refs_4_) | copy-start | bytes 786436 | tf_op jit(solution)/shard_map/cond
  8.0 107.4 %copy-start.4 = (bf16[1,1,8,2,8,512]{5,4,3,2,1,0:T(8,128)(2,1)S(1)}, bf16[1,1,8,2,8,512]{5,4,3,2,1,0:T(8,128)(2,1)}, u32[]{:S(2)}) copy-start(bf16[1,1,8,2,8,512]{5,4,3,2,1,0:T(8,128)(2,1)} %get-tuple-element.88.refs_1_) | copy-start | bytes 393220 | tf_op jit(solution)/shard_map/cond
  8.0 107.3 %copy-start.6 = (bf16[1,1,8,2,8,512]{5,4,3,2,1,0:T(8,128)(2,1)S(1)}, bf16[1,1,8,2,8,512]{5,4,3,2,1,0:T(8,128)(2,1)}, u32[]{:S(2)}) copy-start(bf16[1,1,8,2,8,512]{5,4,3,2,1,0:T(8,128)(2,1)} %get-tuple-element.90.refs_2_) | copy-start | bytes 393220 | tf_op jit(solution)/shard_map/cond
  8.0 107.3 %copy-start.8 = (f32[1,1,8,2,8,8]{5,4,3,2,1,0:T(8,128)S(1)}, f32[1,1,8,2,8,8]{5,4,3,2,1,0:T(8,128)}, u32[]{:S(2)}) copy-start(f32[1,1,8,2,8,8]{5,4,3,2,1,0:T(8,128)} %get-tuple-element.96.refs_5_) | copy-start | bytes 12292 | tf_op jit(solution)/shard_map/cond
  8.0 107.3 %copy-start.10 = (f32[1,1,8,2,8,8]{5,4,3,2,1,0:T(8,128)S(1)}, f32[1,1,8,2,8,8]{5,4,3,2,1,0:T(8,128)}, u32[]{:S(2)}) copy-start(f32[1,1,8,2,8,8]{5,4,3,2,1,0:T(8,128)} %get-tuple-element.98.refs_6_) | copy-start | bytes 12292 | tf_op jit(solution)/shard_map/cond
  8.1 107.3 %copy-start.12 = (f32[128]{0:T(128)S(1)}, f32[128]{0:T(128)}, u32[]{:S(2)}) copy-start(f32[128]{0:T(128)} %get-tuple-element.102) | copy-start | bytes 1540 | tf_op jit(solution)/shard_map/cond

commit v4 on v3

v4 whole, which is shorter than its diff:
```python
import math

import jax
import jax.numpy as jnp
from jax import lax
from jax.experimental import pallas as pl
from jax.experimental.pallas import tpu as pltpu
from jax.sharding import Mesh
from jax.sharding import PartitionSpec as P

SUBGROUPS = 4
SLOT_CAP = 2
CORES = 2
SOURCES = 2
EPS = 1e-06


def pack_kernel(n_group, reqs, spare, placed, states, cells, info, count, sent, sems):
    group = lax.axis_index("group")
    mine = group * SUBGROUPS + lax.axis_index("sub")
    heads = states.shape[1]
    dec_groups = n_group * SUBGROUPS

    def clear(d, carry):
        count[d] = 0
        return carry

    lax.fori_loop(0, dec_groups + dec_groups // CORES, clear, 0, unroll=8)

    def send(r, carry):
        d = placed[group * reqs + r]
        rank = count[d]
        count[d] = rank + 1
        if spare:
            chip = d // CORES
            used = count[dec_groups + chip]
            count[dec_groups + chip] = used + rank
            sent[r] = jnp.where(used * rank == 0, 1, 0)

            @pl.when(rank == 0)
            def _():
                pltpu.make_async_copy(
                    states.at[r], cells.at[d, pl.ds(0, heads)], sems.at[r]
                ).start()

            @pl.when(rank * (1 - used) > 0)
            def _():
                for a in range(heads):
                    pltpu.make_async_copy(
                        states.at[r, a], cells.at[chip * CORES + a, heads], sems.at[r]
                    ).start()

        else:
            pltpu.make_async_copy(states.at[r], cells.at[d, rank], sems.at[r]).start()
        return carry

    lax.fori_loop(0, reqs, send, 0, unroll=4)

    full = 0
    for s in range(n_group):

        def tally(r, sums, s=s):
            live, low, high = sums
            d = placed[s * reqs + r]
            chip = d // CORES
            one = lax.shift_left(1, 4 * (chip % 8))
            live = live + jnp.where(d == mine, 1, 0)
            return live, low + jnp.where(chip < 8, one, 0), high + jnp.where(chip < 8, 0, one)

        live, low, high = lax.fori_loop(0, reqs, tally, (0, 0, 0), unroll=8)
        info[s] = live
        full = full | ((low | high) & 0x44444444)
    info[n_group] = jnp.where(full == 0, 1, 0)

    def drain(r, carry):
        if spare:

            @pl.when(sent[r] > 0)
            def _():
                landed = cells.at[0, pl.ds(0, heads)]
                pltpu.make_async_copy(states.at[r], landed, sems.at[r]).wait()

        else:
            pltpu.make_async_copy(states.at[r], cells.at[0, 0], sems.at[r]).wait()
        return carry

    lax.fori_loop(0, reqs, drain, 0, unroll=4)


def pack(placed, states, n_group, spare):
    reqs, heads, key_size, value_size = states.shape
    cell = (heads + 1,) if spare else (SLOT_CAP, heads)
    dec_groups = n_group * SUBGROUPS
    cells = (dec_groups,) + cell + (key_size, value_size)
    return pl.pallas_call(
        lambda *refs: pack_kernel(n_group, reqs, spare, *refs),
        out_shape=(
            pltpu.VMEM(cells, states.dtype),
            jax.ShapeDtypeStruct((n_group + 1,), jnp.int32),
        ),
        in_specs=[
            pl.BlockSpec(memory_space=pltpu.SMEM),
            pl.BlockSpec(memory_space=pltpu.HBM),
        ],
        out_specs=(
            pl.BlockSpec(memory_space=pltpu.VMEM),
            pl.BlockSpec(memory_space=pltpu.SMEM),
        ),
        scratch_shapes=[
            pltpu.SMEM((dec_groups + dec_groups // CORES,), jnp.int32),
            pltpu.SMEM((reqs,), jnp.int32),
            pltpu.SemaphoreType.DMA((reqs,)),
        ],
        compiler_params=pltpu.CompilerParams(vmem_limit_bytes=32 * 1024 * 1024),
    )(placed, pltpu.with_memory_space_constraint(states, pltpu.HBM))


def split(x):
    high = x.astype(jnp.bfloat16)
    return high, (x - high.astype(jnp.float32)).astype(jnp.bfloat16)


def row_sums(parts):
    rows, lanes = parts[0].shape
    high, low = split(jnp.concatenate(parts, axis=0))
    sums = jnp.dot(
        jnp.concatenate([high, low], axis=1),
        jnp.ones((2 * lanes, lanes), jnp.bfloat16),
        preferred_element_type=jnp.float32,
    )
    return [sums[n * rows : (n + 1) * rows] for n in range(len(parts))]


def widen(columns, width):
    rows, count = columns.shape
    high, rest = split(columns)
    low = columns - high.astype(jnp.float32) - rest.astype(jnp.float32)
    parts = [high.astype(jnp.float32), rest.astype(jnp.float32), low]
    lane = lax.broadcasted_iota(jnp.int32, (count, count * width), 1)
    column = lax.broadcasted_iota(jnp.int32, (count, count * width), 0)
    wide = jnp.dot(
        jnp.concatenate(parts, axis=0).astype(jnp.bfloat16),
        jnp.where(lane // width == column, 1.0, 0.0).astype(jnp.bfloat16),
        preferred_element_type=jnp.float32,
    )
    return wide[:rows] + wide[rows : 2 * rows] + wide[2 * rows :]


def decode_kernel(
    load, chosen, slot, first, live, query, key, value, gate, strength, decay, gain, tokens, states,
    by_key, by_query, values, fades, writes, key_rows, query_rows, kept,
):
    size, width = states.shape[2:]
    heads = states.shape[1] // SUBGROUPS
    steps = key.shape[4]
    units = [(n, i) for n in range(SOURCES) for i in range(SUBGROUPS)]
    count = len(units)

    def keys(i):
        return slice(i * size, (i + 1) * size)

    def lanes(i):
        return slice(i * heads * width, (i + 1) * heads * width)

    def state_of(n, i):
        return jnp.concatenate(
            [states[first + n, heads * i + a] for a in range(heads)]
            if chosen
            else load(first + n, i),
            axis=1,
        )

    def rows(t):
        return slice(t * count, (t + 1) * count)

    def spread(ref, u, x):
        for a in range(heads):
            ref[a, pl.ds(u, steps, stride=count), :] = x[:, a * width : (a + 1) * width]

    def gather(ref, u):
        return jnp.concatenate(
            [ref[a, pl.ds(u, steps, stride=count), :] for a in range(heads)], axis=1
        )

    wide = widen(
        jnp.concatenate(
            [x[0, 0, first + n, slot] for x in (decay, strength) for n in range(SOURCES)], axis=0
        ),
        width,
    )
    for u, (n, i) in enumerate(units):
        key_f = key[0, 0, first + n, slot, :, keys(i)].astype(jnp.float32)
        query_f = query[0, 0, first + n, slot, :, keys(i)].astype(jnp.float32)
        both = jnp.concatenate([key_f, query_f], axis=0).astype(jnp.bfloat16)
        before = load(first + n, i)
        if chosen:
            for a in range(heads):
                states[first + n, heads * i + a] = before[a]
        high, low = split(jnp.concatenate(before, axis=1))
        product = jnp.dot(
            jnp.concatenate([both, both], axis=1),
            jnp.concatenate([high, low], axis=0),
            preferred_element_type=jnp.float32,
        )
        spread(by_key, u, product[:steps])
        spread(by_query, u, product[steps:])
        key_rows[pl.ds(u, steps, stride=count), :] = key_f
        query_rows[pl.ds(u, steps, stride=count), :] = query_f
        spread(values, u, value[0, 0, first + n, slot, :, lanes(i)].astype(jnp.float32))
        spread(fades, u, wide[n * steps : (n + 1) * steps, lanes(i)])
        spread(writes, u, wide[(SOURCES + n) * steps : (SOURCES + n + 1) * steps, lanes(i)])

    on_key = [[by_key[a, rows(t)] for a in range(heads)] for t in range(steps)]
    on_query = [[by_query[a, rows(t)] for a in range(heads)] for t in range(steps)]
    keyed = [key_rows[rows(t)] for t in range(steps)]
    asked = [query_rows[rows(t)] for t in range(steps)]
    pairs = [(l, t) for t in range(steps) for l in range(t, steps)]
    key_key = dict(zip(pairs, row_sums([keyed[l] * keyed[t] for l, t in pairs])))
    query_key = dict(zip(pairs, row_sums([asked[l] * keyed[t] for l, t in pairs])))
    query_norms = [lax.rsqrt(x + EPS) / math.sqrt(size) for x in row_sums([q * q for q in asked])]
    written, total = [], None
    for t in range(steps):
        fade = [fades[a, rows(t)] for a in range(heads)]
        total = fade if total is None else [x * f for x, f in zip(total, fade)]
        norm = lax.rsqrt(key_key[t, t] + EPS)
        write = []
        for a in range(heads):
            residual = values[a, rows(t)] - norm * (on_key[t][a] * fade[a])
            write.append(writes[a, rows(t)] * norm * residual)
        written = [[w * f for w, f in zip(old, fade)] for old in written] + [write]
        for later in range(t, steps):
            for on, dots in ((on_key, key_key), (on_query, query_key)):
                if on is on_query or later > t:
                    dot = dots[later, t]
                    on[later] = [x * f + dot * w for x, f, w in zip(on[later], fade, write)]
    kept[...] = jnp.concatenate(total, axis=1)
    readouts = [x * query_norms[t] for t in range(steps) for x in on_query[t]]
    squares = row_sums([x * x for x in readouts])
    for t in range(steps):
        for a in range(heads):
            by_key[a, rows(t)] = written[t][a]
            norm = lax.rsqrt(squares[t * heads + a] / width + EPS)
            by_query[a, rows(t)] = readouts[t * heads + a] * norm * gain[...]

    for u, (n, i) in enumerate(units):
        key_f = key[0, 0, first + n, slot, :, keys(i)].astype(jnp.float32)
        high, low = split(gather(by_key, u))
        update = lax.dot_general(
            jnp.concatenate([key_f, key_f], axis=0).astype(jnp.bfloat16),
            jnp.concatenate([high.astype(jnp.float32), low.astype(jnp.float32)], axis=0).astype(
                jnp.bfloat16
            ),
            (((0,), (0,)), ((), ())),
            preferred_element_type=jnp.float32,
        )
        state = kept[u : u + 1, :] * state_of(n, i) + update
        for a in range(heads):
            states[first + n, heads * i + a] = state[:, a * width : (a + 1) * width]
        opened = gate[0, 0, first + n, slot, :, lanes(i)].astype(jnp.float32)
        token = gather(by_query, u) * (opened * jax.nn.sigmoid(opened))
        tokens[first + n, :, lanes(i)] = token.astype(tokens.dtype)

    for n in range(SOURCES):

        @pl.when(live[first + n] <= slot)
        def _(n=n):
            tokens[first + n] = jnp.zeros(tokens.shape[1:], tokens.dtype)
            states[first + n] = jnp.zeros(states.shape[1:], states.dtype)


def decode(live, sources, load, slot, small, gain, earlier=None):
    queries, values = small[0], small[2]
    n_group, cap, steps = queries.shape[2:5]
    key_size, value_size = queries.shape[5] // SUBGROUPS, gain.shape[1]
    heads = values.shape[5] // (SUBGROUPS * value_size)
    block = (SUBGROUPS * heads, key_size, value_size)
    units = SOURCES * SUBGROUPS
    rows = steps * units
    by_step = (heads, rows, value_size)
    scratch = [by_step] * 5 + [(rows, key_size)] * 2 + [(units, heads * value_size)]
    kept = () if earlier is None else earlier

    def kernel(live, *refs):
        blocks, refs = refs[: len(sources)], refs[len(sources) :]
        ins, refs = refs[: len(small) + 1], refs[len(small) + 1 :]
        before, refs = refs[: len(kept)], refs[len(kept) :]
        tokens, finals, states, sems, *work = refs
        if kept:
            result, tokens = tokens, work.pop()

        def place(batch):
            span = pl.ds(batch * SOURCES, SOURCES)
            return pltpu.make_async_copy(
                states.at[span], finals.at[0, 0, span, slot], sems.at[batch]
            )

        def run(batch, carry):
            mine = tokens.at[0, 0, :, slot] if kept else tokens
            decode_kernel(
                lambda s, i: load(s, i, *blocks), len(sources) > 1, slot, batch * SOURCES, live,
                *ins, mine, states, *work,
            )
            place(batch).start()
            return carry

        lax.fori_loop(0, n_group // SOURCES, run, 0)
        if kept:
            for s in range(n_group):
                tokens[0, 0, s, 0] = before[0][s]
            copy = pltpu.make_async_copy(tokens, result, sems.at[n_group // SOURCES])
            copy.start()
            copy.wait()
        for batch in range(n_group // SOURCES):
            place(batch).wait()

    vmem, any_space = pl.BlockSpec(memory_space=pltpu.VMEM), pl.BlockSpec(memory_space=pl.ANY)
    in_vmem = [pltpu.with_memory_space_constraint(x, pltpu.VMEM) for x in sources]
    tokens_shape = values.shape if kept else (n_group,) + values.shape[4:]
    return pl.pallas_call(
        kernel,
        out_shape=(
            jax.ShapeDtypeStruct(tokens_shape, jnp.bfloat16),
            jax.ShapeDtypeStruct((1, 1, n_group, cap) + block, jnp.float32),
        ),
        in_specs=[pl.BlockSpec(memory_space=pltpu.SMEM)]
        + [vmem] * (len(sources) + len(small) + 1)
        + [vmem, any_space][: len(kept)],
        out_specs=(any_space if kept else vmem, any_space),
        scratch_shapes=[
            pltpu.VMEM((n_group,) + block, jnp.float32),
            pltpu.SemaphoreType.DMA((n_group // SOURCES + 1,)),
        ]
        + [pltpu.VMEM(shape, jnp.float32) for shape in scratch]
        + [pltpu.VMEM(tokens_shape, jnp.bfloat16)] * bool(kept),
        input_output_aliases={len(sources) + len(small) + 3: 1} if kept else {},
        compiler_params=pltpu.CompilerParams(vmem_limit_bytes=32 * 1024 * 1024),
    )(live, *in_vmem, *small, gain, *kept)


def exchange(cells):
    return lax.all_to_all(cells, ("group", "sub"), split_axis=0, concat_axis=0, tiled=True)


def with_spare(cells, live, placed, states, small, gain, n_group):
    heads, key_size, value_size = states.shape[1:]
    square = (key_size, value_size)
    arrived = exchange(cells)
    spare = arrived[:, heads]
    swap = [(n, n ^ 1) for n in range(SUBGROUPS)]
    other = lax.ppermute(spare, "sub", swap)
    by_source = arrived.reshape((n_group, SUBGROUPS, heads + 1) + square)
    other = other.reshape((n_group, SUBGROUPS) + square)
    earlier = decode(
        live, [by_source], lambda s, i, x: [x[s, i, a] for a in range(heads)], 0, small, gain
    )

    def load(s, i, x, y):
        core = lax.axis_index("sub") % CORES
        return [jnp.where(core == a, x[s, i, heads], y[s, i]) for a in range(heads)]

    return decode(live, [by_source, other], load, 1, small, gain, earlier)


def without_spare(cells, live, placed, states, small, gain, n_group):
    cells, live = pack(placed, states, n_group, False)
    heads, key_size, value_size = states.shape[1:]
    square = (key_size, value_size)
    arrived = exchange(cells).reshape((n_group, SUBGROUPS, SLOT_CAP, heads) + square)
    earlier = None
    for slot in range(SLOT_CAP):
        earlier = decode(
            live,
            [arrived],
            lambda s, i, x, slot=slot: [x[s, i, slot, a] for a in range(heads)],
            slot,
            small,
            gain,
            earlier,
        )
    return earlier


def local(states, placement, queries, key_vectors, value_vectors, gate_inputs, strength, decay, gain):
    n_group = lax.axis_size("group")
    placed = placement.reshape(placement.shape[0])
    cells, info = pack(placed, states, n_group, True)
    small = (queries, key_vectors, value_vectors, gate_inputs, strength, decay)
    gain = gain.reshape(1, gain.shape[0])
    return lax.cond(
        info[n_group] > 0,
        lambda *x: with_spare(*x, n_group),
        lambda *x: without_spare(*x, n_group),
        cells,
        info,
        placed,
        states,
        small,
        gain,
    )


def solution(mesh):
    n_group, n_head = mesh.devices.shape
    quads = Mesh(
        mesh.devices.reshape(n_group, n_head // SUBGROUPS, SUBGROUPS), ("group", "block", "sub")
    )
    spread = P("group", ("block", "sub"))
    return jax.shard_map(
        local,
        mesh=quads,
        in_specs=(spread, P(), spread, spread, spread, spread, spread, spread, P()),
        out_specs=(spread, spread),
        check_vma=False,
    )
```

time: 125 us -> 106 us (0.85)
  blocking collectives: 107 us -> 85 us
  local copies, waits for them, and re-layouts: 0.64 us -> 3.49 us
  other arithmetic: 2.21 us -> 0 us
  Pallas kernels: 13.7 us -> 15.2 us
    all_to_all x1, blocking collectives: 107 us -> 85 us  [exchange(): lax.all_to_all(cells, ('group', 'sub'), split_axis=0, concat_axis=0, tile...]
    unnamed x1 -> x2, local copies, waits for them, and re-layouts: 0.51 us -> 2.65 us
    pallas_call x1, Pallas kernels: 3.88 us -> 5.27 us  [pack(): pl.pallas_call(lambda *refs: pack_kernel(n_group, reqs, spare, *refs), ou...]
    unnamed x1 -> x0, other arithmetic: 1.34 us -> none
    pallas_call x1 -> x2, Pallas kernels: 9.83 us -> 9.98 us  [decode(): pl.pallas_call(kernel, out_shape=(jax.ShapeDtypeStruct(tokens_shape, jnp....]
  transfers between devices with their start and end apart: 0 -> 1, of which waited for: 0 -> 0; matrix products, arithmetic and copies ran while one was open for 0% -> 0% of each run, Pallas kernels for 0% -> 5%
where the time goes in v4:
time: 106 us; the launch traced here: 105 us
  blocking collectives  85 us (80%)
  Pallas kernels  15.2 us (14%)
  local copies, waits for them, and re-layouts  3.49 us (3%)
  between operations  1.3 us (1%)
    all_to_all x1, blocking collectives, exchange(): lax.all_to_all(cells, ('group', 'sub'), split_axis=0, concat_axis=0, tile...  85 us
    pallas_call x2, Pallas kernels, decode(): pl.pallas_call(kernel, out_shape=(jax.ShapeDtypeStruct(tokens_shape, jnp....  9.98 us
    pallas_call x1, Pallas kernels, pack(): pl.pallas_call(lambda *refs: pack_kernel(n_group, reqs, spare, *refs), ou...  5.27 us
    unnamed x2, local copies, waits for them, and re-layouts  2.65 us
  transfers between devices with their start and end apart: 1, of which 0 were waited for; matrix products, arithmetic and copies ran while one was open for 0% of the time, Pallas kernels for 5%

profile of v4, /device:TPU:1, one launch (start us, length us, event | category | flops | bytes accessed | tf_op | source)
XLA Modules:
  0.0 105.3 jit_solution(3855272114264395076)
XLA Ops:
  0.6 5.3 %shard_map.108 = (f32[32,3,128,128]{3,2,1,0:T(8,128)S(1)}, s32[9]{0:T(128)S(1)}) custom-call(s32[256]{0:T(256)} %bitcast.15, f32[32,2,128,128]{3,2,1,0:T(8,128)} %refs_1_.1), custom_call_target="tpu_custom_call" | custom-call | tf_op jit(solution)/shard_map/pallas_call | solution.py:95
  5.9 0.0 copy-start
  5.9 2.6 %copy-done = f32[32,3,128,128]{3,2,1,0:T(8,128)} copy-done((f32[32,3,128,128]{3,2,1,0:T(8,128)}, f32[32,3,128,128]{3,2,1,0:T(8,128)S(1)}, u32[]{:S(2)}) %copy-start) | copy-done | bytes 6291480
  8.6 0.6 slice.6
  9.8 95.5 %conditional.1 = ((bf16[1,1,8,2,8,1024]{5,4,3,2,1,0:T(8,128)(2,1)}, f32[1,1,8,2,8,128,128]{6,5,4,3,2,1,0:T(8,128)})) conditional(s32[]{:T(128)} %bitcast.5, (s32[256]{0:T(256)}, f32[32,2,128,128]{3,2,1,0:T(8,128)}, bf16[1,1,8,2,8,512]{5,4,3,2,1,0:T(8,128)(2,1)}, bf16[1,1,8,2,8,512]{5,4,3,2,1,0:T(8,128)(2,1)}, ...), branch_computations={%region_0.0_spmd, %region_1.0_spmd} | conditional | bytes 28346612 | solution.py:389
  9.8 0.0 copy-start.2
  9.8 0.0 copy-start.4
  9.8 0.0 copy-start.6
  9.9 0.0 copy-start.8
  9.9 0.0 copy-start.10
  9.9 0.0 copy-start.12
  9.9 0.0 copy-start.14
  9.9 85.0 %all_to_all.9 = f32[32,3,128,128]{3,2,1,0:T(8,128)S(1)} all-to-all(f32[32,3,128,128]{3,2,1,0:T(8,128)} %get-tuple-element.50), channel_id=1, replica_groups=mesh['group'=8,'block'=4,'sub'=4] {'group','sub'}, dimensions={0} | all-to-all | bytes 12582912 | tf_op jit(solution)/shard_map/cond/branch_1_fun/all_to_all | solution.py:341
  94.9 0.2 slice_bitcast_fusion
  95.2 0.1 collective-permute-start
  95.2 0.0 copy-done.2
  95.3 0.0 copy-done.4
  95.3 0.0 copy-done.6
  95.3 0.0 copy-done.8
  95.3 0.0 copy-done.10
  95.3 0.0 copy-done.12
  95.3 0.0 copy-done.14
  95.3 4.7 %branch_1_fun.2 = (bf16[8,8,1024]{2,1,0:T(8,128)(2,1)S(1)}, f32[1,1,8,2,8,128,128]{6,5,4,3,2,1,0:T(8,128)}) custom-call(s32[9]{0:T(128)S(1)} %get-tuple-element.49.live, f32[8,4,3,128,128]{4,3,2,1,0:T(8,128)S(1)} %bitcast.10, bf16[1,1,8,2,8,512]{5,4,3,2,1,0:T(8,128)(2,1)S(1)} %copy-done.6, bf16[1,1,8,2,8,512]{5,4,3,2,1,0:T(8,128)(2,1)S(1)} %copy-done.8, ...), custom_call_target="tpu_custom_call" | custom-call | tf_op jit(solution)/shard_map/cond/branch_1_fun/pallas_call | solution.py:319
  100.1 0.0 collective-permute-done
  100.1 5.2 %branch_1_fun.3 = (bf16[1,1,8,2,8,1024]{5,4,3,2,1,0:T(8,128)(2,1)}, f32[1,1,8,2,8,128,128]{6,5,4,3,2,1,0:T(8,128)}) custom-call(s32[9]{0:T(128)S(1)} %get-tuple-element.49.live, f32[8,4,3,128,128]{4,3,2,1,0:T(8,128)S(1)} %bitcast.11, f32[8,4,128,128]{3,2,1,0:T(8,128)S(1)} %bitcast.12, ...), custom_call_target="tpu_custom_call", output_to_operand_aliasing={{1}: (11, {})} | custom-call | tf_op jit(solution)/shard_map/cond/branch_1_fun/pallas_call | solution.py:319
Async XLA Ops:
  5.9 2.7 %copy-start = (f32[32,3,128,128]{3,2,1,0:T(8,128)}, f32[32,3,128,128]{3,2,1,0:T(8,128)S(1)}, u32[]{:S(2)}) copy-start(f32[32,3,128,128]{3,2,1,0:T(8,128)S(1)} %get-tuple-element.65) | copy-start | bytes 18874372
  9.8 85.4 %copy-start.2 = (bf16[1,1,8,2,8,1024]{5,4,3,2,1,0:T(8,128)(2,1)S(1)}, bf16[1,1,8,2,8,1024]{5,4,3,2,1,0:T(8,128)(2,1)}, u32[]{:S(2)}) copy-start(bf16[1,1,8,2,8,1024]{5,4,3,2,1,0:T(8,128)(2,1)} %get-tuple-element.53.refs_3_.refs_4_) | copy-start | bytes 786436 | tf_op jit(solution)/shard_map/cond
  9.8 85.4 %copy-start.4 = (bf16[1,1,8,2,8,1024]{5,4,3,2,1,0:T(8,128)(2,1)S(1)}, bf16[1,1,8,2,8,1024]{5,4,3,2,1,0:T(8,128)(2,1)}, u32[]{:S(2)}) copy-start(bf16[1,1,8,2,8,1024]{5,4,3,2,1,0:T(8,128)(2,1)} %get-tuple-element.54.refs_4_.refs_5_) | copy-start | bytes 786436 | tf_op jit(solution)/shard_map/cond
  9.8 85.4 %copy-start.6 = (bf16[1,1,8,2,8,512]{5,4,3,2,1,0:T(8,128)(2,1)S(1)}, bf16[1,1,8,2,8,512]{5,4,3,2,1,0:T(8,128)(2,1)}, u32[]{:S(2)}) copy-start(bf16[1,1,8,2,8,512]{5,4,3,2,1,0:T(8,128)(2,1)} %get-tuple-element.51.refs_1_.refs_2_) | copy-start | bytes 393220 | tf_op jit(solution)/shard_map/cond
  9.9 85.4 %copy-start.8 = (bf16[1,1,8,2,8,512]{5,4,3,2,1,0:T(8,128)(2,1)S(1)}, bf16[1,1,8,2,8,512]{5,4,3,2,1,0:T(8,128)(2,1)}, u32[]{:S(2)}) copy-start(bf16[1,1,8,2,8,512]{5,4,3,2,1,0:T(8,128)(2,1)} %get-tuple-element.52.refs_2_.refs_3_) | copy-start | bytes 393220 | tf_op jit(solution)/shard_map/cond
  9.9 85.4 %copy-start.10 = (f32[1,1,8,2,8,8]{5,4,3,2,1,0:T(8,128)S(1)}, f32[1,1,8,2,8,8]{5,4,3,2,1,0:T(8,128)}, u32[]{:S(2)}) copy-start(f32[1,1,8,2,8,8]{5,4,3,2,1,0:T(8,128)} %get-tuple-element.55.refs_5_.refs_6_) | copy-start | bytes 12292 | tf_op jit(solution)/shard_map/cond
  9.9 85.4 %copy-start.12 = (f32[1,1,8,2,8,8]{5,4,3,2,1,0:T(8,128)S(1)}, f32[1,1,8,2,8,8]{5,4,3,2,1,0:T(8,128)}, u32[]{:S(2)}) copy-start(f32[1,1,8,2,8,8]{5,4,3,2,1,0:T(8,128)} %get-tuple-element.56.refs_6_.refs_7_) | copy-start | bytes 12292 | tf_op jit(solution)/shard_map/cond
  9.9 85.4 %copy-start.14 = (f32[1,128]{1,0:T(1,128)S(1)}, f32[1,128]{1,0:T(1,128)}, u32[]{:S(2)}) copy-start(f32[1,128]{1,0:T(1,128)} %get-tuple-element.57.refs_7_.refs_8_) | copy-start | bytes 1540 | tf_op jit(solution)/shard_map/cond
  95.2 4.9 %collective-permute-start = (f32[32,128,128]{2,1,0:T(8,128)S(1)}, f32[32,128,128]{2,1,0:T(8,128)S(1)}, u32[]{:S(2)}, u32[]{:S(2)}) collective-permute-start(f32[32,128,128]{2,1,0:T(8,128)S(1)} %slice_bitcast_fusion), channel_id=1, source_target_pairs={{0,1},{1,0},{2,3},{3,2},{4,5},{5,4},{6,7},{7,6},{8,9},{9,8},{10,11... | collective-permute-start | bytes 6291464 | tf_op jit(solution)/shard_map/cond/branch_1_fun/ppermute | solution.py:350

commit v5 on v4

--- a/solution.py
+++ b/solution.py
@@ -15,27 +15,45 @@
 EPS = 1e-06
 
 
-def pack_kernel(n_group, reqs, spare, placed, states, cells, info, count, sent, sems):
+def fits_kernel(dec_groups, reqs, placed, fits):
+    lanes = placed.shape[1]
+    chips = placed[...] // CORES
+    named = [jnp.where(chips == chip, 1.0, 0.0) for chip in range(dec_groups // CORES)]
+    lane = lax.broadcasted_iota(jnp.int32, (lanes, lanes), 0)
+    group = lax.broadcasted_iota(jnp.int32, (lanes, lanes), 1)
+    counts = jnp.dot(
+        jnp.concatenate(named, axis=0).astype(jnp.bfloat16),
+        jnp.where(lane // reqs == group, 1.0, 0.0).astype(jnp.bfloat16),
+        preferred_element_type=jnp.float32,
+    )
+    fits[0] = jnp.where(jnp.max(counts) < SLOT_CAP + 1.5, 1, 0)
+
+
+def cells_fit(placed, dec_groups, reqs):
+    return pl.pallas_call(
+        lambda *refs: fits_kernel(dec_groups, reqs, *refs),
+        out_shape=jax.ShapeDtypeStruct((1,), jnp.int32),
+        in_specs=[pl.BlockSpec(memory_space=pltpu.VMEM)],
+        out_specs=pl.BlockSpec(memory_space=pltpu.SMEM),
+    )(placed.reshape(-1, 128))
+
+
+def pack_kernel(n_group, reqs, spare, placed, states, cells, live, count, sems):
     group = lax.axis_index("group")
     mine = group * SUBGROUPS + lax.axis_index("sub")
     heads = states.shape[1]
-    dec_groups = n_group * SUBGROUPS
 
     def clear(d, carry):
         count[d] = 0
         return carry
 
-    lax.fori_loop(0, dec_groups + dec_groups // CORES, clear, 0, unroll=8)
+    lax.fori_loop(0, n_group * SUBGROUPS, clear, 0, unroll=8)
 
     def send(r, carry):
         d = placed[group * reqs + r]
         rank = count[d]
         count[d] = rank + 1
         if spare:
-            chip = d // CORES
-            used = count[dec_groups + chip]
-            count[dec_groups + chip] = used + rank
-            sent[r] = jnp.where(used * rank == 0, 1, 0)
 
             @pl.when(rank == 0)
             def _():
@@ -43,11 +61,11 @@
                     states.at[r], cells.at[d, pl.ds(0, heads)], sems.at[r]
                 ).start()
 
-            @pl.when(rank * (1 - used) > 0)
+            @pl.when(rank > 0)
             def _():
                 for a in range(heads):
                     pltpu.make_async_copy(
-                        states.at[r, a], cells.at[chip * CORES + a, heads], sems.at[r]
+                        states.at[r, a], cells.at[d // CORES * CORES + a, heads], sems.at[r]
                     ).start()
 
         else:
@@ -56,32 +74,16 @@
 
     lax.fori_loop(0, reqs, send, 0, unroll=4)
 
-    full = 0
     for s in range(n_group):
 
-        def tally(r, sums, s=s):
-            live, low, high = sums
-            d = placed[s * reqs + r]
-            chip = d // CORES
-            one = lax.shift_left(1, 4 * (chip % 8))
-            live = live + jnp.where(d == mine, 1, 0)
-            return live, low + jnp.where(chip < 8, one, 0), high + jnp.where(chip < 8, 0, one)
-
-        live, low, high = lax.fori_loop(0, reqs, tally, (0, 0, 0), unroll=8)
-        info[s] = live
-        full = full | ((low | high) & 0x44444444)
-    info[n_group] = jnp.where(full == 0, 1, 0)
+        def tally(r, total, s=s):
+            return total + jnp.where(placed[s * reqs + r] == mine, 1, 0)
+
+        live[s] = lax.fori_loop(0, reqs, tally, 0, unroll=8)
 
     def drain(r, carry):
-        if spare:
-
-            @pl.when(sent[r] > 0)
-            def _():
-                landed = cells.at[0, pl.ds(0, heads)]
-                pltpu.make_async_copy(states.at[r], landed, sems.at[r]).wait()
-
-        else:
-            pltpu.make_async_copy(states.at[r], cells.at[0, 0], sems.at[r]).wait()
+        landed = cells.at[0, pl.ds(0, heads)] if spare else cells.at[0, 0]
+        pltpu.make_async_copy(states.at[r], landed, sems.at[r]).wait()
         return carry
 
     lax.fori_loop(0, reqs, drain, 0, unroll=4)
@@ -90,13 +92,12 @@
 def pack(placed, states, n_group, spare):
     reqs, heads, key_size, value_size = states.shape
     cell = (heads + 1,) if spare else (SLOT_CAP, heads)
-    dec_groups = n_group * SUBGROUPS
-    cells = (dec_groups,) + cell + (key_size, value_size)
+    cells = (n_group * SUBGROUPS,) + cell + (key_size, value_size)
     return pl.pallas_call(
         lambda *refs: pack_kernel(n_group, reqs, spare, *refs),
         out_shape=(
             pltpu.VMEM(cells, states.dtype),
-            jax.ShapeDtypeStruct((n_group + 1,), jnp.int32),
+            jax.ShapeDtypeStruct((n_group,), jnp.int32),
         ),
         in_specs=[
             pl.BlockSpec(memory_space=pltpu.SMEM),
@@ -107,8 +108,7 @@
             pl.BlockSpec(memory_space=pltpu.SMEM),
         ),
         scratch_shapes=[
-            pltpu.SMEM((dec_groups + dec_groups // CORES,), jnp.int32),
-            pltpu.SMEM((reqs,), jnp.int32),
+            pltpu.SMEM((n_group * SUBGROUPS,), jnp.int32),
             pltpu.SemaphoreType.DMA((reqs,)),
         ],
         compiler_params=pltpu.CompilerParams(vmem_limit_bytes=32 * 1024 * 1024),
@@ -341,7 +341,8 @@
     return lax.all_to_all(cells, ("group", "sub"), split_axis=0, concat_axis=0, tiled=True)
 
 
-def with_spare(cells, live, placed, states, small, gain, n_group):
+def with_spare(placed, states, small, gain, n_group):
+    cells, live = pack(placed, states, n_group, True)
     heads, key_size, value_size = states.shape[1:]
     square = (key_size, value_size)
     arrived = exchange(cells)
@@ -361,7 +362,7 @@
     return decode(live, [by_source, other], load, 1, small, gain, earlier)
 
 
-def without_spare(cells, live, placed, states, small, gain, n_group):
+def without_spare(placed, states, small, gain, n_group):
     cells, live = pack(placed, states, n_group, False)
     heads, key_size, value_size = states.shape[1:]
     square = (key_size, value_size)
@@ -383,15 +384,13 @@
 def local(states, placement, queries, key_vectors, value_vectors, gate_inputs, strength, decay, gain):
     n_group = lax.axis_size("group")
     placed = placement.reshape(placement.shape[0])
-    cells, info = pack(placed, states, n_group, True)
+    fits = cells_fit(placed, n_group * SUBGROUPS, states.shape[0])
     small = (queries, key_vectors, value_vectors, gate_inputs, strength, decay)
     gain = gain.reshape(1, gain.shape[0])
     return lax.cond(
-        info[n_group] > 0,
+        fits[0] > 0,
         lambda *x: with_spare(*x, n_group),
         lambda *x: without_spare(*x, n_group),
-        cells,
-        info,
         placed,
         states,
         small,

time: 106 us -> 102 us (0.962)
  local copies, waits for them, and re-layouts: 3.49 us -> 0.26 us
    unnamed x2 -> x0, local copies, waits for them, and re-layouts: 2.65 us -> none
    pallas_call x0 -> x1, Pallas kernels: none -> 1.45 us  [cells_fit(): pl.pallas_call(lambda *refs: fits_kernel(dec_groups, reqs, *refs), out_sh...]
    pallas_call x1, Pallas kernels: 5.27 us -> 3.86 us  [pack(): pl.pallas_call(lambda *refs: pack_kernel(n_group, reqs, spare, *refs), ou...]
where the time goes in v5:
time: 102 us
  blocking collectives  84.8 us (83%)
  Pallas kernels  15.3 us (15%)
  between operations  1.29 us (1%)
    all_to_all x1, blocking collectives, exchange(): lax.all_to_all(cells, ('group', 'sub'), split_axis=0, concat_axis=0, tile...  84.8 us
    pallas_call x2, Pallas kernels, decode(): pl.pallas_call(kernel, out_shape=(jax.ShapeDtypeStruct(tokens_shape, jnp....  10 us
    pallas_call x1, Pallas kernels, pack(): pl.pallas_call(lambda *refs: pack_kernel(n_group, reqs, spare, *refs), ou...  3.86 us
  transfers between devices with their start and end apart: 1, of which 0 were waited for; matrix products, arithmetic and copies ran while one was open for 0% of the time, Pallas kernels for 5%

profile of v5, /device:TPU:1, one launch (start us, length us, event | category | flops | bytes accessed | tf_op | source)
XLA Modules:
  0.0 102.0 jit_solution(10705236047426345500)
XLA Ops:
  0.6 1.5 %shard_map.124 = s32[1]{0:T(128)} custom-call(s32[2,128]{1,0:T(2,128)} %bitcast.20), custom_call_target="tpu_custom_call" | custom-call | tf_op jit(solution)/shard_map/pallas_call | solution.py:33
  2.7 99.2 %conditional.1 = ((bf16[1,1,8,2,8,1024]{5,4,3,2,1,0:T(8,128)(2,1)}, f32[1,1,8,2,8,128,128]{6,5,4,3,2,1,0:T(8,128)})) conditional(s32[]{:T(128)} %bitcast.9, (s32[256,1]{0,1:T(1,128)}, f32[32,2,128,128]{3,2,1,0:T(8,128)}, bf16[1,1,8,2,8,512]{5,4,3,2,1,0:T(8,128)(2,1)}, bf16[1,1,8,2,8,512]{5,4,3,2,1,0:T(8,128)(2,1)}, ...), branch_computations={%region_0.0_spmd, %region_1.0_spmd} | conditional | bytes 28346612 | solution.py:390
  2.8 3.9 %branch_1_fun.3 = (f32[32,3,128,128]{3,2,1,0:T(8,128)S(1)}, s32[8]{0:T(128)S(1)}) custom-call(s32[256]{0:T(256)} %bitcast.22, f32[32,2,128,128]{3,2,1,0:T(8,128)} %get-tuple-element.89.refs_1_), custom_call_target="tpu_custom_call" | custom-call | tf_op jit(solution)/shard_map/cond/branch_1_fun/pallas_call | solution.py:96
  6.6 0.0 copy-start.1
  6.6 0.0 copy-start.3
  6.7 0.0 copy-start.5
  6.7 0.0 copy-start.7
  6.7 0.0 copy-start.9
  6.7 0.0 copy-start.11
  6.7 0.0 copy-start.13
  6.7 84.8 %all_to_all.9 = f32[32,3,128,128]{3,2,1,0:T(8,128)S(1)} all-to-all(f32[32,3,128,128]{3,2,1,0:T(8,128)S(1)} %get-tuple-element.52), channel_id=1, replica_groups=mesh['group'=8,'block'=4,'sub'=4] {'group','sub'}, dimensions={0} | all-to-all | bytes 12582912 | tf_op jit(solution)/shard_map/cond/branch_1_fun/all_to_all | solution.py:341
  91.5 0.2 slice_bitcast_fusion
  91.8 0.1 collective-permute-start
  91.9 0.0 copy-done.1
  91.9 0.0 copy-done.3
  91.9 0.0 copy-done.5
  91.9 0.0 copy-done.7
  91.9 0.0 copy-done.9
  91.9 0.0 copy-done.11
  91.9 0.0 copy-done.13
  91.9 4.7 %branch_1_fun.4 = (bf16[8,8,1024]{2,1,0:T(8,128)(2,1)S(1)}, f32[1,1,8,2,8,128,128]{6,5,4,3,2,1,0:T(8,128)}) custom-call(s32[8]{0:T(128)S(1)} %get-tuple-element.51.live, f32[8,4,3,128,128]{4,3,2,1,0:T(8,128)S(1)} %bitcast.13, bf16[1,1,8,2,8,512]{5,4,3,2,1,0:T(8,128)(2,1)S(1)} %copy-done.5, bf16[1,1,8,2,8,512]{5,4,3,2,1,0:T(8,128)(2,1)S(1)} %copy-done.7, ...), custom_call_target="tpu_custom_call" | custom-call | tf_op jit(solution)/shard_map/cond/branch_1_fun/pallas_call | solution.py:319
  96.7 0.0 collective-permute-done
  96.7 5.3 %branch_1_fun.5 = (bf16[1,1,8,2,8,1024]{5,4,3,2,1,0:T(8,128)(2,1)}, f32[1,1,8,2,8,128,128]{6,5,4,3,2,1,0:T(8,128)}) custom-call(s32[8]{0:T(128)S(1)} %get-tuple-element.51.live, f32[8,4,3,128,128]{4,3,2,1,0:T(8,128)S(1)} %bitcast.14, f32[8,4,128,128]{3,2,1,0:T(8,128)S(1)} %bitcast.15, ...), custom_call_target="tpu_custom_call", output_to_operand_aliasing={{1}: (11, {})} | custom-call | tf_op jit(solution)/shard_map/cond/branch_1_fun/pallas_call | solution.py:319
Async XLA Ops:
  6.6 85.2 %copy-start.1 = (bf16[1,1,8,2,8,1024]{5,4,3,2,1,0:T(8,128)(2,1)S(1)}, bf16[1,1,8,2,8,1024]{5,4,3,2,1,0:T(8,128)(2,1)}, u32[]{:S(2)}) copy-start(bf16[1,1,8,2,8,1024]{5,4,3,2,1,0:T(8,128)(2,1)} %get-tuple-element.95.refs_3_.refs_4_) | copy-start | bytes 786436 | tf_op jit(solution)/shard_map/cond
  6.6 85.2 %copy-start.3 = (bf16[1,1,8,2,8,1024]{5,4,3,2,1,0:T(8,128)(2,1)S(1)}, bf16[1,1,8,2,8,1024]{5,4,3,2,1,0:T(8,128)(2,1)}, u32[]{:S(2)}) copy-start(bf16[1,1,8,2,8,1024]{5,4,3,2,1,0:T(8,128)(2,1)} %get-tuple-element.97.refs_4_.refs_5_) | copy-start | bytes 786436 | tf_op jit(solution)/shard_map/cond
  6.7 85.2 %copy-start.5 = (bf16[1,1,8,2,8,512]{5,4,3,2,1,0:T(8,128)(2,1)S(1)}, bf16[1,1,8,2,8,512]{5,4,3,2,1,0:T(8,128)(2,1)}, u32[]{:S(2)}) copy-start(bf16[1,1,8,2,8,512]{5,4,3,2,1,0:T(8,128)(2,1)} %get-tuple-element.91.refs_1_.refs_2_) | copy-start | bytes 393220 | tf_op jit(solution)/shard_map/cond
  6.7 85.2 %copy-start.7 = (bf16[1,1,8,2,8,512]{5,4,3,2,1,0:T(8,128)(2,1)S(1)}, bf16[1,1,8,2,8,512]{5,4,3,2,1,0:T(8,128)(2,1)}, u32[]{:S(2)}) copy-start(bf16[1,1,8,2,8,512]{5,4,3,2,1,0:T(8,128)(2,1)} %get-tuple-element.93.refs_2_.refs_3_) | copy-start | bytes 393220 | tf_op jit(solution)/shard_map/cond
  6.7 85.2 %copy-start.9 = (f32[1,1,8,2,8,8]{5,4,3,2,1,0:T(8,128)S(1)}, f32[1,1,8,2,8,8]{5,4,3,2,1,0:T(8,128)}, u32[]{:S(2)}) copy-start(f32[1,1,8,2,8,8]{5,4,3,2,1,0:T(8,128)} %get-tuple-element.99.refs_5_.refs_6_) | copy-start | bytes 12292 | tf_op jit(solution)/shard_map/cond
  6.7 85.2 %copy-start.11 = (f32[1,1,8,2,8,8]{5,4,3,2,1,0:T(8,128)S(1)}, f32[1,1,8,2,8,8]{5,4,3,2,1,0:T(8,128)}, u32[]{:S(2)}) copy-start(f32[1,1,8,2,8,8]{5,4,3,2,1,0:T(8,128)} %get-tuple-element.101.refs_6_.refs_7_) | copy-start | bytes 12292 | tf_op jit(solution)/shard_map/cond
  6.7 85.2 %copy-start.13 = (f32[128]{0:T(128)S(1)}, f32[128]{0:T(128)}, u32[]{:S(2)}) copy-start(f32[128]{0:T(128)} %get-tuple-element.105) | copy-start | bytes 1540 | tf_op jit(solution)/shard_map/cond
  91.8 4.9 %collective-permute-start = (f32[32,128,128]{2,1,0:T(8,128)S(1)}, f32[32,128,128]{2,1,0:T(8,128)S(1)}, u32[]{:S(2)}, u32[]{:S(2)}) collective-permute-start(f32[32,128,128]{2,1,0:T(8,128)S(1)} %slice_bitcast_fusion), channel_id=1, source_target_pairs={{0,1},{1,0},{2,3},{3,2},{4,5},{5,4},{6,7},{7,6},{8,9},{9,8},{10,11... | collective-permute-start | bytes 6291464 | tf_op jit(solution)/shard_map/cond/branch_1_fun/ppermute | solution.py:351
